TPU v7x, 128 devices: a whole 4x4x4 slice. The times are simulated.
128 devices in a mesh: prow: 16 (over z, x), pcol: 8 (over y, core).
Axes of the slice: x: 4, y: 4, z: 4, core: 2. Of those that a mesh axis runs over, the one named last changes fastest.
Arguments:
- panel: float32 [16384, 128], P('prow'), may hold values from -1.3268871 to 11.326887
- trailing: float32 [16384, 16384], P('prow', 'pcol'), may hold values from -8 to 8
Outputs:
- updated: float32 [16384, 16384], P('prow', 'pcol')
- band_block: float32 [128, 128], replicated
All inputs are finite; a program needn't handle non-finite values.
Results may differ from a plain program's by a relative error of at most 0.00012.
Values sent between devices are 32-bit elements; how exact they have to be, the bound alone decides.
No kernel may reach another device: no remote copies, remote signals or barrier semaphores. Data moves between devices by JAX's collectives and lax.ppermute only.
A program may use at most 128 MiB of HBM per device.

v0:
```python
import jax
import jax.numpy as jnp
from jax import lax
from jax.sharding import PartitionSpec as P

PANEL = 128


def from_everyone(value, axis):
    copies = jnp.broadcast_to(value, (lax.axis_size(axis), *value.shape))
    return lax.all_to_all(copies, axis, split_axis=0, concat_axis=0, tiled=True)


def over_copies(value, axis):
    return from_everyone(value, axis).sum(axis=0)


def packed_total(arrays, axis):
    ends = [0]
    for a in arrays:
        ends.append(ends[-1] + a.size)
    total = over_copies(jnp.concatenate([a.ravel() for a in arrays]), axis)
    return tuple((total[b:e].reshape(a.shape) for a, b, e in zip(arrays, ends, ends[1:])))


def hdot(left, right):
    return jnp.dot(left, right, precision=lax.Precision.HIGHEST, preferred_element_type=jnp.float32)


def shards(panel, trailing):
    local_rows = panel.shape[0]
    local_cols = trailing.shape[1]
    row_place = lax.axis_index("prow")
    col_place = lax.axis_index("pcol")
    gram_local = hdot(panel.T, panel)
    masked = jnp.where(row_place == 0, panel[:PANEL], jnp.zeros_like(panel[:PANEL]))
    gram, top_rows = packed_total((gram_local, masked), "prow")
    lower = jnp.linalg.cholesky(gram)
    basis = jax.scipy.linalg.solve_triangular(lower, panel.T, lower=True).T
    head = jax.scipy.linalg.solve_triangular(lower, top_rows.T, lower=True).T
    identity_mat = jnp.eye(PANEL, dtype=jnp.float32)
    shifted = identity_mat + head.T
    normal_mat = hdot(shifted.T, shifted)
    normal_factor = jnp.linalg.cholesky(normal_mat)
    coupling = jax.scipy.linalg.cho_solve((normal_factor, True), shifted.T)
    global_rows = row_place * local_rows + jnp.arange(local_rows, dtype=jnp.int32)
    unit = (global_rows[:, None] == jnp.arange(PANEL, dtype=jnp.int32)[None, :]).astype(jnp.float32)
    vectors = basis + unit
    col_start = col_place * local_cols
    gathered = lax.all_gather(vectors, "prow", axis=0, tiled=True)
    col_vectors = lax.dynamic_slice_in_dim(gathered, col_start, local_cols, 0)
    product = over_copies(hdot(trailing, col_vectors), "pcol")
    mixed = hdot(product, coupling)
    small = hdot(coupling.T, over_copies(hdot(vectors.T, mixed), "prow"))
    update = mixed - 0.5 * hdot(vectors, small)
    col_partial = lax.dot_general(
        trailing,
        vectors,
        (((0,), (0,)), ((), ())),
        precision=lax.Precision.HIGHEST,
        preferred_element_type=jnp.float32,
    )
    col_product = lax.psum(col_partial, "prow")
    col_update = hdot(col_product, coupling) - 0.5 * hdot(col_vectors, small)
    updated = trailing - hdot(vectors, col_update.T) - hdot(update, col_vectors.T)
    return (updated, -lower.T)


def solution(mesh):
    placed = (P("prow", None), P("prow", "pcol"))
    return jax.shard_map(
        shards, mesh=mesh, in_specs=placed, out_specs=(P("prow", "pcol"), P()), check_vma=False
    )
```

profile of v0, /device:TPU:1, one launch (start us, length us, event | category | flops | bytes accessed | tf_op | source)
XLA Modules:
  0.0 322.8 jit_solution(8266819011205010898)
XLA Ops:
  7.2 2.3 convolution_bitcast_fusion.1
  9.4 0.8 select_bitcast_fusion.1
  10.3 2.9 broadcast_in_dim.16
  13.2 8.4 %all-to-all-start = ((f32[16,1,32768]{2,1,0:T(1,128)}), f32[16,1,32768]{2,1,0:T(1,128)S(1)}, u32[]{:S(2)}, u32[]{:S(2)}) async-start(f32[16,1,32768]{2,1,0:T(1,128)} %broadcast_in_dim.16), calls=%async_computation | async-start | bytes 4194304 | tf_op jit(solution)/shard_map/all_to_all | solution.py:11
  22.3 29.9 %all-to-all-done = f32[16,1,32768]{2,1,0:T(1,128)S(1)} async-done(((f32[16,1,32768]{2,1,0:T(1,128)}), f32[16,1,32768]{2,1,0:T(1,128)S(1)}, u32[]{:S(2)}, u32[]{:S(2)}) %all-to-all-start) | async-done | bytes 2097184 | tf_op jit(solution)/shard_map/all_to_all | solution.py:11
  52.2 1.4 reduce_sum.27
  53.7 11.7 %cholesky.44 = f32[128,128]{1,0:T(8,128)S(1)} custom-call(f32[128,128]{1,0:T(8,128)S(1)} %fusion.15), custom_call_target="Cholesky" | custom-call | tf_op jit(solution)/shard_map/jit(cholesky)/cholesky | solution.py:38
  65.4 0.6 compare_reduce_fusion.1
  66.1 0.7 negate_bitcast_fusion
  66.7 9.8 %custom-call.13 = f32[1,128,128]{1,2,0:T(8,128)S(1)} custom-call(f32[1,128,128]{2,1,0:T(8,128)S(1)} %get-tuple-element.13), custom_call_target="InvertDiagBlocksLowerTriangular" | custom-call | tf_op jit(solution)/shard_map/jit(_solve_triangular)/triangular_solve | solution.py:39
  76.6 1.5 fusion.1
  78.1 70.5 %all-gather.2.cloned.1.call-done = f32[16384,128]{0,1:T(8,128)} async-done(((f32[1024,128]{0,1:T(8,128)}), f32[16384,128]{0,1:T(8,128)}) %all-gather.2.cloned.1.call-update) | async-done | bytes 8388624 | tf_op jit(solution)/shard_map/all_gather | solution.py:50
  148.6 11.4 %convolution_bitcast_fusion.2 = f32[1024,128]{0,1:T(8,128)S(1)} fusion(f32[1024,2048]{1,0:T(8,128)} %param.6, f32[16384,128]{0,1:T(8,128)} %all-gather.2.cloned.1.call-done, s32[]{:T(128)S(6)} %select_n.16), kind=kOutput, calls=%fused_computation.5 | convolution fusion | flops 3221225472 | bytes 9961476 | tf_op jit(solution)/shard_map/dot_general | solution.py:27
  160.2 2.3 broadcast_in_dim.17
  162.5 5.3 %all-to-all-start.1 = ((f32[8,1024,128]{2,1,0:T(8,128)}), f32[8,1024,128]{2,1,0:T(8,128)}, u32[]{:S(2)}, u32[]{:S(2)}) async-start(f32[8,1024,128]{2,1,0:T(8,128)} %broadcast_in_dim.17), calls=%async_computation.1 | async-start | bytes 8388608 | tf_op jit(solution)/shard_map/all_to_all | solution.py:11
  168.5 11.7 %cholesky.55 = f32[128,128]{1,0:T(8,128)S(1)} custom-call(f32[128,128]{1,0:T(8,128)S(1)} %fusion.12), custom_call_target="Cholesky" | custom-call | tf_op jit(solution)/shard_map/jit(cholesky)/cholesky | solution.py:44
  180.2 0.6 compare_reduce_fusion
  180.9 0.7 fusion.6
  181.5 9.8 %custom-call.14 = f32[1,128,128]{1,2,0:T(8,128)S(1)} custom-call(f32[1,128,128]{2,1,0:T(8,128)S(1)} %fusion.6), custom_call_target="InvertDiagBlocksLowerTriangular" | custom-call | tf_op jit(solution)/shard_map/jit(_cho_solve)/triangular_solve | solution.py:45
  191.4 7.8 %convolution_bitcast_fusion = f32[2048,128]{0,1:T(8,128)} fusion(f32[1024,128]{0,1:T(8,128)S(1)} %copy-done, f32[1024,2048]{1,0:T(8,128)} %param.6), kind=kOutput, calls=%fused_computation.1 | convolution fusion | flops 3221225472 | bytes 9961472 | tf_op jit(solution)/shard_map/dot_general | solution.py:56
  199.7 17.0 %all-to-all-done.1 = f32[8,1024,128]{2,1,0:T(8,128)} async-done(((f32[8,1024,128]{2,1,0:T(8,128)}), f32[8,1024,128]{2,1,0:T(8,128)}, u32[]{:S(2)}, u32[]{:S(2)}) %all-to-all-start.1) | async-done | bytes 4194336 | tf_op jit(solution)/shard_map/all_to_all | solution.py:11
  216.7 2.5 reduce_sum.28
  219.8 0.6 fusion.23
  220.4 1.1 broadcast_in_dim.18
  221.5 5.2 %all-to-all-start.2 = ((f32[16,128,128]{2,1,0:T(8,128)}), f32[16,128,128]{2,1,0:T(8,128)S(1)}, u32[]{:S(2)}, u32[]{:S(2)}) async-start(f32[16,128,128]{2,1,0:T(8,128)} %broadcast_in_dim.18), calls=%async_computation.2 | async-start | bytes 2097152 | tf_op jit(solution)/shard_map/all_to_all | solution.py:11
  226.7 0.7 copy.20
  227.5 62.2 %all-reduce.2.cloned.1.call-done = f32[2048,128]{0,1:T(8,128)} async-done(((f32[2048,128]{0,1:T(8,128)}), f32[2048,128]{0,1:T(8,128)}) %all-reduce.2.cloned.1.call-update) | async-done | bytes 1048592 | tf_op jit(solution)/shard_map/psum | solution.py:63
  289.7 3.0 fusion.21
  293.1 1.0 fusion.2
  294.1 3.2 fusion
  297.3 7.1 %fusion.25 = f32[1024,2048]{1,0:T(8,128)S(1)} fusion(f32[1024,128]{0,1:T(8,128)S(1)} %copy-done, f32[2048,128]{1,0:T(8,128)S(1)} %fusion), kind=kOutput, calls=%fused_computation.51 | convolution fusion | flops 3221225472 | bytes 9961472 | tf_op jit(solution)/shard_map/dot_general | solution.py:27
  304.4 11.3 %subtract_subtract_fusion = f32[1024,2048]{1,0:T(8,128)} fusion(f32[1024,2048]{1,0:T(8,128)S(1)} %bitcast.76, f32[1024,2048]{1,0:T(8,128)S(1)} %fusion.25, f32[1024,128]{1,0:T(8,128)S(1)} %fusion.2, f32[16384,128]{0,1:T(8,128)} %all-gather.2.cloned.1.call-done, s32[]{:T(128)S(6)} %select_n.16), kind=kOutput, calls=%fused_computation | convolution fusion | flops 3225419776 | bytes 26738692 | tf_op jit(solution)/shard_map/dot_general | solution.py:27
  (31 shorter events, 3.1 us)
Async XLA Ops:
  7.2 69.4 %copy-start.1 = (f32[1024,128]{1,0:T(8,128)S(1)}, f32[1024,128]{1,0:T(8,128)}, u32[]{:S(2)}) copy-start(f32[1024,128]{1,0:T(8,128)} %param.5) | copy-start | bytes 1572868
  13.2 38.9 %all-to-all-start = ((f32[16,1,32768]{2,1,0:T(1,128)}), f32[16,1,32768]{2,1,0:T(1,128)S(1)}, u32[]{:S(2)}, u32[]{:S(2)}) async-start(f32[16,1,32768]{2,1,0:T(1,128)} %broadcast_in_dim.16), calls=%async_computation | async-start | bytes 4194304 | tf_op jit(solution)/shard_map/all_to_all | solution.py:11
  21.7 126.9 %all-gather.2.cloned.1.call-start = ((), (), s32[]{:S(2)}) async-start(), calls=%async_computation.4 | async-start | bytes 8912896 | tf_op jit(solution)/shard_map/all_gather | solution.py:50
  160.0 31.4 %copy-start = (f32[1024,128]{0,1:T(8,128)S(1)}, f32[1024,128]{0,1:T(8,128)}, u32[]{:S(2)}) copy-start(f32[1024,128]{0,1:T(8,128)} %fusion.1) | copy-start | bytes 1572868
  162.5 54.3 %all-to-all-start.1 = ((f32[8,1024,128]{2,1,0:T(8,128)}), f32[8,1024,128]{2,1,0:T(8,128)}, u32[]{:S(2)}, u32[]{:S(2)}) async-start(f32[8,1024,128]{2,1,0:T(8,128)} %broadcast_in_dim.17), calls=%async_computation.1 | async-start | bytes 8388608 | tf_op jit(solution)/shard_map/all_to_all | solution.py:11
  167.8 121.9 %all-reduce.2.cloned.1.call-start = ((), (), s32[]{:S(2)}) async-start(), calls=%async_computation.3 | async-start | bytes 2097152 | tf_op jit(solution)/shard_map/psum | solution.py:63
  221.5 71.2 %all-to-all-start.2 = ((f32[16,128,128]{2,1,0:T(8,128)}), f32[16,128,128]{2,1,0:T(8,128)S(1)}, u32[]{:S(2)}, u32[]{:S(2)}) async-start(f32[16,128,128]{2,1,0:T(8,128)} %broadcast_in_dim.18), calls=%async_computation.2 | async-start | bytes 2097152 | tf_op jit(solution)/shard_map/all_to_all | solution.py:11
  294.1 10.3 %slice-start = ((s8[8388608]{0:T(1024)(128)(4,1)}), s8[4194304]{0:T(1024)(128)(4,1)S(1)}, s32[]{:S(2)}) async-start(s8[8388608]{0:T(1024)(128)(4,1)} %bitcast.75), calls=%async_computation.5 | async-start | bytes 8388608
  297.3 7.1 %slice-start.1 = ((s8[8388608]{0:T(1024)(128)(4,1)}), s8[4194304]{0:T(1024)(128)(4,1)S(1)}, s32[]{:S(2)}) async-start(s8[8388608]{0:T(1024)(128)(4,1)} %bitcast.75), calls=%async_computation.6 | async-start | bytes 8388608
Sparse Core Ops, SparseCore 0:
  78.2 70.3 all-gather.1
  199.3 90.2 all-reduce.1
where the time goes:
time: 327 us; the launch traced here: 323 us
  waiting for transfers between devices  180 us (55%)
  matrix products  51.1 us (16%)
  other arithmetic  50.5 us (15%)
  starting transfers between devices  19.5 us (6%)
  between operations  14.6 us (4%)
  local copies, waits for them, and re-layouts  7.43 us (2%)
    all_gather x1, waiting for transfers between devices, shards(): gathered = lax.all_gather(vectors, 'prow', axis=0, tiled=True)  70.5 us
    psum x1, waiting for transfers between devices, shards(): col_product = lax.psum(col_partial, 'prow')  62.2 us
    all_to_all x3, waiting for transfers between devices, from_everyone(): return lax.all_to_all(copies, axis, split_axis=0, concat_axis=0, tiled=True)  46.9 us
    dot_general x11, matrix products, hdot(): jnp.dot(left, right, precision=lax.Precision.HIGHEST, preferred_element_t...  41 us
    all_to_all x3, starting transfers between devices, from_everyone(): return lax.all_to_all(copies, axis, split_axis=0, concat_axis=0, tiled=True)  19 us
    another operation x3, other arithmetic, shards(): lower = jnp.linalg.cholesky(gram)  12.4 us
    another operation x3, other arithmetic, shards(): normal_factor = jnp.linalg.cholesky(normal_mat)  12.4 us
    another operation x2, other arithmetic, shards(): coupling = jax.scipy.linalg.cho_solve((normal_factor, True), shifted.T)  10.5 us
  transfers between devices with their start and end apart: 5, of which 4 were waited for; matrix products, arithmetic and copies ran while one was open for 13% of the time, Pallas kernels for 0%

commit v1 on v0

v1 whole, which is shorter than its diff:
```python
import functools

import jax
import jax.numpy as jnp
from jax import lax
from jax.experimental import pallas as pl
from jax.experimental.pallas import tpu as pltpu
from jax.sharding import PartitionSpec as P

B = 128
ZN, XN, YN, CN = 4, 4, 4, 2
F32, BF16 = jnp.float32, jnp.bfloat16
VMEM_LIMIT = 48 * 1024 * 1024


def hdot(left, right, dims=((1,), (0,))):
    return lax.dot_general(
        left, right, (dims, ((), ())), precision=lax.Precision.HIGHEST, preferred_element_type=F32
    )


def bdot(left, right, dims=((1,), (0,))):
    return lax.dot_general(left, right, (dims, ((), ())), preferred_element_type=F32)


def split(value):
    high = value.astype(BF16)
    return high, (value - high.astype(F32)).astype(BF16)


def iotas(shape=(B, B)):
    return lax.broadcasted_iota(jnp.int32, shape, 0), lax.broadcasted_iota(jnp.int32, shape, 1)


def eye():
    r, c = iotas()
    return jnp.where(r == c, 1.0, 0.0).astype(F32)


def params(**kw):
    return pltpu.CompilerParams(vmem_limit_bytes=VMEM_LIMIT, **kw)


STEPS = 6


def inverse_factor(gram, out_ref, s_ref, x_ref):
    r, c = iotas()
    one = eye()
    diag_row = jnp.sum(one * gram, axis=0, keepdims=True)
    diag_col = jnp.sum(one * gram, axis=1, keepdims=True)
    scale_row, scale_col = lax.rsqrt(diag_row), lax.rsqrt(diag_col)
    corr = gram * scale_row * scale_col
    x = one
    err = corr - one
    for step in range(STEPS):
        if step:
            err = hdot(hdot(x, corr), x, ((1,), (1,))) - one
        phi = jnp.where(r > c, err, jnp.where(r == c, 0.5 * err, 0.0))
        x = x - (phi if step == 0 else hdot(phi, x))
    out_ref[...] = x * scale_row
    size = jnp.sum(err * err)
    good = size < 1e-8

    @pl.when(jnp.logical_not(good))
    def _():
        s_ref[...] = corr
        x_ref[...] = one

        def body(k, carry):
            row = s_ref[pl.ds(k, 1), :]
            rr, cc = iotas()
            ident = rr == cc
            lane = lax.broadcasted_iota(jnp.int32, (1, B), 1)
            pivot = jnp.sum(jnp.where(lane == k, row, 0.0), axis=1, keepdims=True)
            inv = lax.rsqrt(pivot)
            row = row * inv
            col = jnp.sum(jnp.where(ident, jnp.broadcast_to(row, (B, B)), 0.0), axis=1, keepdims=True)
            below = lax.broadcasted_iota(jnp.int32, (B, 1), 0) > k
            col = jnp.where(below, col, 0.0)
            xrow = x_ref[pl.ds(k, 1), :] * inv
            x_ref[pl.ds(k, 1), :] = xrow
            s_ref[...] = s_ref[...] - col * row
            x_ref[...] = x_ref[...] - col * xrow
            return carry

        lax.fori_loop(0, B, body, 0)
        out_ref[...] = x_ref[...] * scale_row


def gram_kernel(panel, row_place):
    def body(place_ref, p_ref, out_ref):
        p = p_ref[...]
        out_ref[:, :B] = hdot(p, p, ((0,), (0,)))
        out_ref[:, B:] = jnp.where(place_ref[0] == 0, p[:B], 0.0)

    return pl.pallas_call(
        body,
        out_shape=jax.ShapeDtypeStruct((B, 2 * B), F32),
        in_specs=[pl.BlockSpec(memory_space=pltpu.SMEM), pl.BlockSpec(memory_space=pltpu.VMEM)],
        out_specs=pl.BlockSpec(memory_space=pltpu.VMEM),
        compiler_params=params(),
        name="gram",
    )(row_place, panel)


def product_kernel(panel, trailing):
    rows, cols = trailing.shape
    tile = 256

    def body(p_ref, a_ref, out_ref, ph_ref):
        @pl.when(pl.program_id(0) == 0)
        def _():
            high, low = split(p_ref[...].T)
            ph_ref[:B], ph_ref[B:] = high, low

        ah, al = split(a_ref[...])
        both = bdot(ph_ref[...], ah)
        z = both[:B] + (both[B:] + bdot(ph_ref[:B], al))
        for k in range(tile // B):
            out_ref[k] = z[:, k * B : (k + 1) * B]

    return pl.pallas_call(
        body,
        grid=(cols // tile,),
        out_shape=jax.ShapeDtypeStruct((cols // B, B, B), F32),
        in_specs=[
            pl.BlockSpec((rows, B), lambda t: (0, 0)),
            pl.BlockSpec((rows, tile), lambda t: (0, t)),
        ],
        out_specs=pl.BlockSpec((tile // B, B, B), lambda t: (t, 0, 0)),
        scratch_shapes=[pltpu.VMEM((2 * B, rows), BF16)],
        compiler_params=params(),
        cost_estimate=pl.CostEstimate(flops=6 * rows * cols * B, bytes_accessed=4 * rows * cols, transcendentals=0),
        name="product",
    )(panel, trailing)


def factor_kernel(parts):
    def body(a_ref, b_ref, c_ref, d_ref, band_ref, rinv_ref, head_ref, linv_ref, s_ref, x_ref):
        total = (a_ref[...] + c_ref[...]) + (b_ref[...] + d_ref[...])
        gram, top = total[:, :B], total[:, B:]
        inverse_factor(gram, linv_ref, s_ref, x_ref)
        linv = linv_ref[...]
        rinv = linv.T
        rinv_ref[...] = rinv
        head_ref[...] = hdot(top, rinv)
        r, c = iotas()
        upper = hdot(linv, gram)
        band_ref[...] = jnp.where(r <= c, -upper, -0.0)

    square = jax.ShapeDtypeStruct((B, B), F32)
    return pl.pallas_call(
        body,
        out_shape=(square, square, square),
        scratch_shapes=[pltpu.VMEM((B, B), F32)] * 3,
        compiler_params=params(),
        name="factor",
    )(*parts)


def coupling_kernel(head):
    def body(h_ref, out_ref, linv_ref, s_ref, x_ref):
        m = eye() + h_ref[...].T
        inverse_factor(hdot(m, m, ((0,), (0,))), linv_ref, s_ref, x_ref)
        linv = linv_ref[...]
        out_ref[...] = hdot(linv, hdot(linv, m, ((1,), (1,))), ((0,), (0,)))

    return pl.pallas_call(
        body,
        out_shape=jax.ShapeDtypeStruct((B, B), F32),
        scratch_shapes=[pltpu.VMEM((B, B), F32)] * 3,
        compiler_params=params(),
        name="coupling",
    )(head)


def chunk_kernel(pieces, pa, rinv, first):
    def body(first_ref, y_ref, pa_ref, r_ref, wv_ref, s_ref):
        total = y_ref[0]
        for k in range(1, y_ref.shape[0]):
            total = total + y_ref[k]
        rinv = r_ref[...]
        w = hdot(total, rinv, ((0,), (0,))) + pa_ref[:, B:]
        v = hdot(pa_ref[:, :B], rinv) + jnp.where(first_ref[0] == 1, eye(), 0.0)
        wv_ref[:, :B] = w
        wv_ref[:, B:] = v
        s_ref[...] = hdot(v, w, ((0,), (0,)))

    vm = pl.BlockSpec(memory_space=pltpu.VMEM)
    return pl.pallas_call(
        body,
        out_shape=(jax.ShapeDtypeStruct((B, 2 * B), F32), jax.ShapeDtypeStruct((B, B), F32)),
        in_specs=[pl.BlockSpec(memory_space=pltpu.SMEM), vm, vm, vm],
        out_specs=(vm, vm),
        compiler_params=params(),
        name="chunk",
    )(first, pieces, pa, rinv)


def left_kernel(panel, w_rows, rinv, coupling, s_a, s_b, row_place):
    rows = panel.shape[0]

    def body(place_ref, p_ref, w_ref, r_ref, t_ref, sa_ref, sb_ref, hi_ref, lo_ref):
        t = t_ref[...]
        small = hdot(hdot(t, sa_ref[...] + sb_ref[...], ((0,), (0,))), t)
        small = 0.5 * (small + small.T)
        r, c = iotas((rows, B))
        unit = jnp.where((r == c) & (place_ref[0] == 0), 1.0, 0.0)
        v = hdot(p_ref[...], r_ref[...]) + unit
        hi_ref[:, :B], lo_ref[:, :B] = split(hdot(v, t, ((1,), (1,))))
        hi_ref[:, B:], lo_ref[:, B:] = split(hdot(w_ref[...], t) - hdot(v, small))

    vm = pl.BlockSpec(memory_space=pltpu.VMEM)
    half = jax.ShapeDtypeStruct((rows, 2 * B), BF16)
    return pl.pallas_call(
        body,
        out_shape=(half, half),
        in_specs=[pl.BlockSpec(memory_space=pltpu.SMEM)] + [vm] * 6,
        out_specs=(vm, vm),
        compiler_params=params(),
        name="left",
    )(row_place, panel, w_rows, rinv, coupling, s_a, s_b)


def update_kernel(trailing, high, low, right):
    rows, cols = trailing.shape
    tile = 256

    def body(a_ref, h_ref, l_ref, r_ref, out_ref):
        rh, rl = split(r_ref[...])
        h = h_ref[...]
        nt = ((1,), (1,))
        out_ref[...] = a_ref[...] - (bdot(h, rh, nt) + (bdot(h, rl, nt) + bdot(l_ref[...], rh, nt)))

    whole = pl.BlockSpec((rows, 2 * B), lambda t: (0, 0))
    return pl.pallas_call(
        body,
        grid=(cols // tile,),
        out_shape=jax.ShapeDtypeStruct((rows, cols), F32),
        in_specs=[
            pl.BlockSpec((rows, tile), lambda t: (0, t)),
            whole,
            whole,
            pl.BlockSpec((tile, 2 * B), lambda t: (t, 0)),
        ],
        out_specs=pl.BlockSpec((rows, tile), lambda t: (0, t)),
        compiler_params=params(),
        cost_estimate=pl.CostEstimate(flops=12 * rows * cols * B, bytes_accessed=8 * rows * cols, transcendentals=0),
        name="update",
    )(trailing, high, low, right)


def along_x(d):
    return [(z * XN + x, z * XN + (x + d) % XN) for z in range(ZN) for x in range(XN)]


def along_z(d):
    return [(z * XN + x, (z + d) % ZN * XN + x) for z in range(ZN) for x in range(XN)]


def along_y(d):
    return [(y * CN + c, (y + d) % YN * CN + c) for y in range(YN) for c in range(CN)]


def along_c(d):
    return [(y * CN + c, y * CN + (c + d) % CN) for y in range(YN) for c in range(CN)]


def four(value, axis, along):
    return [value] + [lax.ppermute(value, axis, along(d)) for d in (1, 2, 3)]


def add_four(parts):
    return (parts[0] + parts[2]) + (parts[1] + parts[3])


def shards(panel, trailing):
    rows, cols = trailing.shape
    prow, pcol = lax.axis_size("prow"), lax.axis_size("pcol")
    i, j = lax.axis_index("prow"), lax.axis_index("pcol")
    row_place = i.astype(jnp.int32).reshape(1)
    first = ((i == 0) & (j == 0)).astype(jnp.int32).reshape(1)
    per_row = rows // B
    ratio = cols // rows

    spread = []
    for a in range(prow):
        for k in range(per_row):
            spread.append((a * pcol + k, (per_row * (a % ratio) + k) * pcol + a // ratio))
    gather = [(d, s) for s, d in spread]

    parts = four(gram_kernel(panel, row_place), "prow", along_x)
    parts = four(add_four(parts), "prow", along_z)

    z = product_kernel(panel, trailing)
    pieces = lax.all_to_all(z, "prow", split_axis=0, concat_axis=0, tiled=True)

    lead = trailing[:, :B].reshape(YN, CN, B, B)
    held = jnp.where(j == 0, lead[:, 0], lax.ppermute(lead[:, 1], "pcol", [(0, 1)]))
    sent = [lax.ppermute(held[y], "pcol", [(c, y * CN + c) for c in range(CN)]) for y in range(1, YN)]
    ae = jnp.where(j < CN, held[0], sent[0] + sent[1] + sent[2])
    mine = lax.dynamic_slice_in_dim(panel, j * B, B, 0)
    pa = lax.ppermute(jnp.concatenate([mine, ae], axis=1), ("prow", "pcol"), spread)

    band, rinv, head = factor_kernel(parts)
    wv, s = chunk_kernel(pieces, pa, rinv, first)

    copies = jnp.broadcast_to(wv, (prow, B, 2 * B))
    right = lax.all_to_all(copies, "prow", split_axis=0, concat_axis=0, tiled=True).reshape(cols, 2 * B)
    w_row = lax.ppermute(wv[:, :B], ("prow", "pcol"), gather)
    copies = jnp.broadcast_to(w_row, (pcol, B, B))
    w_rows = lax.all_to_all(copies, "pcol", split_axis=0, concat_axis=0, tiled=True).reshape(rows, B)

    coupling = coupling_kernel(head)
    s = add_four(four(s, "prow", along_x))
    s = add_four(four(s, "prow", along_z))
    s = add_four(four(s, "pcol", along_y))
    s_other = lax.ppermute(s, "pcol", along_c(1))
    high, low = left_kernel(panel, w_rows, rinv, coupling, s, s_other, row_place)
    return update_kernel(trailing, high, low, right), band


def solution(mesh):
    placed = (P("prow", None), P("prow", "pcol"))
    return jax.shard_map(
        shards, mesh=mesh, in_specs=placed, out_specs=(P("prow", "pcol"), P()), check_vma=False
    )
```

time: 327 us -> 182 us (0.56); the launches traced: 323 us -> 181 us
  waiting for transfers between devices: 180 us -> 38.2 us
  Pallas kernels: 0 us -> 55.5 us
  matrix products: 51.1 us -> 0 us
  other arithmetic: 50.5 us -> 0.15 us
  starting transfers between devices: 19.5 us -> 59.4 us
  blocking collectives: 0 us -> 19.7 us
  between operations: 14.6 us -> 0.91 us
    all_gather x1 -> x0, waiting for transfers between devices: 70.5 us -> none  [shards(): gathered = lax.all_gather(vectors, 'prow', axis=0, tiled=True)]
    psum x1 -> x0, waiting for transfers between devices: 62.2 us -> none  [shards(): col_product = lax.psum(col_partial, 'prow')]
    pallas_call x0 -> x7, Pallas kernels: none -> 55.5 us  [the longest x1 27.9 us: factor_kernel(): pl.pallas_call(body, out_shape=(square, square, square), scratch_shapes=[...]
    dot_general x12 -> x0, matrix products: 48.8 us -> none  [the longest x11 41 us: hdot(): jnp.dot(left, right, precision=lax.Precision.HIGHEST, preferred_element_t...]
    all_to_all x3 -> x2, waiting for transfers between devices: 46.9 us -> 0.01 us  [the longest x1 0.01 us: shards(): lax.all_to_all(copies, 'prow', split_axis=0, concat_axis=0, tiled=True)]
    another operation x9 -> x0, other arithmetic: 45 us -> none  [the longest x3 12.4 us: shards(): lower = jnp.linalg.cholesky(gram)]
    ppermute x0 -> x22, starting transfers between devices: none -> 44.8 us  [the longest x15 20.8 us: four(): return [value] + [lax.ppermute(value, axis, along(d)) for d in (1, 2, 3)]]
    ppermute x0 -> x22, waiting for transfers between devices: none -> 38.2 us  [the longest x15 36.9 us: four(): return [value] + [lax.ppermute(value, axis, along(d)) for d in (1, 2, 3)]]
  transfers between devices with their start and end apart: 5 -> 24, of which waited for: 4 -> 9; matrix products, arithmetic and copies ran while one was open for 13% -> 1% of each run, Pallas kernels for 0% -> 24%
where the time goes in v1:
time: 182 us; the launch traced here: 181 us
  starting transfers between devices  59.4 us (33%)
  Pallas kernels  55.5 us (30%)
  waiting for transfers between devices  38.2 us (21%)
  blocking collectives  19.7 us (11%)
  local copies, waits for them, and re-layouts  7.39 us (4%)
    ppermute x15, waiting for transfers between devices, four(): return [value] + [lax.ppermute(value, axis, along(d)) for d in (1, 2, 3)]  36.9 us
    pallas_call x1, Pallas kernels, factor_kernel(): pl.pallas_call(body, out_shape=(square, square, square), scratch_shapes=[...  27.9 us
    ppermute x15, starting transfers between devices, four(): return [value] + [lax.ppermute(value, axis, along(d)) for d in (1, 2, 3)]  20.8 us
    all_to_all x1, blocking collectives, shards(): lax.all_to_all(copies, 'pcol', split_axis=0, concat_axis=0, tiled=True)  19.7 us
    pallas_call x1, Pallas kernels, update_kernel(): pl.pallas_call(body, grid=(cols // tile,), out_shape=jax.ShapeDtypeStruct...  10.6 us
    pallas_call x1, Pallas kernels, product_kernel(): pl.pallas_call(body, grid=(cols // tile,), out_shape=jax.ShapeDtypeStruct...  8.31 us
    all_to_all x1, starting transfers between devices, shards(): lax.all_to_all(copies, 'prow', split_axis=0, concat_axis=0, tiled=True)  8.17 us
    ppermute x3, starting transfers between devices, shards(): lax.ppermute(held[y], 'pcol', [(c, y * CN + c) for c in range(CN)])  6.79 us
  transfers between devices with their start and end apart: 24, of which 9 were waited for; matrix products, arithmetic and copies ran while one was open for 1% of the time, Pallas kernels for 24%

profile of v1, /device:TPU:1, one launch (start us, length us, event | category | flops | bytes accessed | tf_op | source)
XLA Modules:
  0.0 181.2 jit_solution(13090543329069173511)
XLA Ops:
  2.3 3.4 %collective-permute-start.7 = (f32[128,256]{1,0:T(8,128)S(1)}, f32[128,256]{1,0:T(8,128)S(1)}, u32[]{:S(2)}, u32[]{:S(2)}) collective-permute-start(f32[128,256]{1,0:T(8,128)S(1)} %gram.1), channel_id=1, source_target_pairs={{0,24},{8,0},{16,8},{24,16},{32,56},{40,32},{48,40},{56,48},{64,88... | collective-permute-start | bytes 393224 | tf_op jit(solution)/shard_map/ppermute | solution.py:271
  5.7 1.7 collective-permute-start.5
  7.4 1.1 slice.24
  8.5 1.3 collective-permute-start
  9.8 8.3 %product.1 = f32[16,128,128]{2,1,0:T(8,128)} custom-call(f32[1024,128]{1,0:T(8,128)S(1)} %copy-done, f32[1024,2048]{1,0:T(8,128)} %a_ref.3), custom_call_target="tpu_custom_call" | custom-call | flops 1610612736 | bytes 8388608 | tf_op jit(solution)/shard_map/product/pallas_call | solution.py:123
  18.2 6.4 %all-to-all-start = ((f32[16,128,128]{2,1,0:T(8,128)}), f32[16,128,128]{2,1,0:T(8,128)S(1)}, u32[]{:S(2)}, u32[]{:S(2)}) async-start(f32[16,128,128]{2,1,0:T(8,128)} %product.1), calls=%async_computation | async-start | bytes 2097152 | tf_op jit(solution)/shard_map/all_to_all | solution.py:297
  24.6 4.2 %collective-permute-start.2 = (f32[128,128]{1,0:T(8,128)S(1)}, f32[128,128]{1,0:T(8,128)S(1)}, u32[]{:S(2)}, u32[]{:S(2)}) collective-permute-start(f32[128,128]{1,0:T(8,128)S(1)} %get-tuple-element.16), channel_id=1, source_target_pairs={{0,4},{1,5},{8,12},{9,13},{16,20},{17,21},{24,28},{25,29},{32,36},... | collective-permute-start | bytes 196616 | tf_op jit(solution)/shard_map/ppermute | solution.py:301
  28.8 1.3 collective-permute-start.3
  30.2 1.3 collective-permute-start.1
  31.5 2.6 %collective-permute-start.10 = (f32[128,256]{1,0:T(8,128)S(1)}, f32[128,256]{1,0:T(8,128)S(1)}, u32[]{:S(2)}, u32[]{:S(2)}) collective-permute-start(f32[128,256]{1,0:T(8,128)S(1)} %add_add_fusion.a_ref), channel_id=1, source_target_pairs={{0,96},{8,104},{16,112},{24,120},{32,0},{40,8},{48,16},{56,24},{64... | collective-permute-start | bytes 393224 | tf_op jit(solution)/shard_map/ppermute | solution.py:271
  35.4 6.2 %collective-permute-start.4 = (f32[128,256]{1,0:T(8,128)S(1)}, f32[128,256]{1,0:T(8,128)S(1)}, u32[]{:S(2)}, u32[]{:S(2)}) collective-permute-start(f32[128,256]{1,0:T(8,128)S(1)} %pad_maximum_fusion), channel_id=1, source_target_pairs={{0,0},{1,8},{2,16},{3,24},{4,32},{5,40},{6,48},{7,56},{8,64},{9,72... | collective-permute-start | bytes 393224 | tf_op jit(solution)/shard_map/ppermute | solution.py:304
  41.8 4.4 %collective-permute-done.8.b_ref = f32[128,256]{1,0:T(8,128)S(1)} collective-permute-done((f32[128,256]{1,0:T(8,128)S(1)}, f32[128,256]{1,0:T(8,128)S(1)}, u32[]{:S(2)}, u32[]{:S(2)}) %collective-permute-start.8) | collective-permute-done | bytes 131104 | tf_op jit(solution)/shard_map/ppermute | solution.py:271
  46.2 27.9 %factor.1 = (f32[128,128]{1,0:T(8,128)}, f32[128,128]{1,0:T(8,128)S(1)}, f32[128,128]{1,0:T(8,128)S(1)}) custom-call(f32[128,256]{1,0:T(8,128)S(1)} %add_add_fusion.a_ref, f32[128,256]{1,0:T(8,128)S(1)} %collective-permute-done.8.b_ref, f32[128,256]{1,0:T(8,128)S(1)} %collective-permute-done.9.c_ref, f32[128,256]{1,0:T(8,128)S(1)} %collective-permute-done.10.d_ref), custom_call_target="tpu_custom_call" | custom-call | tf_op jit(solution)/shard_map/factor/pallas_call | solution.py:153
  74.8 4.2 %collective-permute-start.11 = (f32[128,128]{1,0:T(8,128)S(1)}, f32[128,128]{1,0:T(8,128)S(1)}, u32[]{:S(2)}, u32[]{:S(2)}) collective-permute-start(f32[128,128]{1,0:T(8,128)S(1)} %slice.31), channel_id=1, source_target_pairs={{0,0},{8,1},{16,2},{24,3},{32,4},{40,5},{48,6},{56,7},{64,8},{72,9... | collective-permute-start | bytes 196616 | tf_op jit(solution)/shard_map/ppermute | solution.py:311
  79.1 1.3 collective-permute-done.11
  80.4 19.7 %all_to_all.15 = f32[8,128,128]{2,1,0:T(8,128)S(1)} all-to-all(f32[8,128,128]{2,1,0:T(8,128)S(1)} %broadcast_in_dim.6), channel_id=1, replica_groups=mesh['prow'=16,'pcol'=8] {'pcol'}, dimensions={0} | all-to-all | bytes 1048576 | tf_op jit(solution)/shard_map/all_to_all | solution.py:313
  100.1 1.5 broadcast_in_dim.7
  101.6 8.2 %all-to-all-start.2 = ((f32[16,128,256]{2,1,0:T(8,128)}), f32[16,128,256]{2,1,0:T(8,128)S(1)}, u32[]{:S(2)}, u32[]{:S(2)}) async-start(f32[16,128,256]{2,1,0:T(8,128)} %broadcast_in_dim.7), calls=%async_computation.2 | async-start | bytes 4194304 | tf_op jit(solution)/shard_map/all_to_all | solution.py:310
  109.8 2.6 %collective-permute-start.14 = (f32[128,128]{1,0:T(8,128)S(1)}, f32[128,128]{1,0:T(8,128)S(1)}, u32[]{:S(2)}, u32[]{:S(2)}) collective-permute-start(f32[128,128]{1,0:T(8,128)S(1)} %get-tuple-element.12), channel_id=1, source_target_pairs={{0,24},{8,0},{16,8},{24,16},{32,56},{40,32},{48,40},{56,48},{64,88... | collective-permute-start | bytes 196616 | tf_op jit(solution)/shard_map/ppermute | solution.py:271
  112.4 1.8 collective-permute-start.12
  114.2 23.3 %collective-permute-done.14 = f32[128,128]{1,0:T(8,128)S(1)} collective-permute-done((f32[128,128]{1,0:T(8,128)S(1)}, f32[128,128]{1,0:T(8,128)S(1)}, u32[]{:S(2)}, u32[]{:S(2)}) %collective-permute-start.14) | collective-permute-done | bytes 65568 | tf_op jit(solution)/shard_map/ppermute | solution.py:271
  138.0 2.8 %collective-permute-done.12 = f32[128,128]{1,0:T(8,128)S(1)} collective-permute-done((f32[128,128]{1,0:T(8,128)S(1)}, f32[128,128]{1,0:T(8,128)S(1)}, u32[]{:S(2)}, u32[]{:S(2)}) %collective-permute-start.12) | collective-permute-done | bytes 65568 | tf_op jit(solution)/shard_map/ppermute | solution.py:271
  140.9 1.8 %collective-permute-start.17 = (f32[128,128]{1,0:T(8,128)S(1)}, f32[128,128]{1,0:T(8,128)S(1)}, u32[]{:S(2)}, u32[]{:S(2)}) collective-permute-start(f32[128,128]{1,0:T(8,128)S(1)} %add_add_fusion.3), channel_id=1, source_target_pairs={{0,96},{8,104},{16,112},{24,120},{32,0},{40,8},{48,16},{56,24},{64... | collective-permute-start | bytes 196616 | tf_op jit(solution)/shard_map/ppermute | solution.py:271
  142.7 2.3 %collective-permute-start.15 = (f32[128,128]{1,0:T(8,128)S(1)}, f32[128,128]{1,0:T(8,128)S(1)}, u32[]{:S(2)}, u32[]{:S(2)}) collective-permute-start(f32[128,128]{1,0:T(8,128)S(1)} %add_add_fusion.3), channel_id=1, source_target_pairs={{0,64},{8,72},{16,80},{24,88},{32,96},{40,104},{48,112},{56,120},{... | collective-permute-start | bytes 196616 | tf_op jit(solution)/shard_map/ppermute | solution.py:271
  145.0 2.7 %collective-permute-done.16 = f32[128,128]{1,0:T(8,128)S(1)} collective-permute-done((f32[128,128]{1,0:T(8,128)S(1)}, f32[128,128]{1,0:T(8,128)S(1)}, u32[]{:S(2)}, u32[]{:S(2)}) %collective-permute-start.16) | collective-permute-done | bytes 65568 | tf_op jit(solution)/shard_map/ppermute | solution.py:271
  149.3 1.9 %collective-permute-start.18 = (f32[128,128]{1,0:T(8,128)S(1)}, f32[128,128]{1,0:T(8,128)S(1)}, u32[]{:S(2)}, u32[]{:S(2)}) collective-permute-start(f32[128,128]{1,0:T(8,128)S(1)} %add_add_fusion.2), channel_id=1, source_target_pairs={{0,4},{1,5},{2,6},{3,7},{4,0},{5,1},{6,2},{7,3},{8,12},{9,13},{10,... | collective-permute-start | bytes 196616 | tf_op jit(solution)/shard_map/ppermute | solution.py:271
  151.2 1.9 %collective-permute-done.19 = f32[128,128]{1,0:T(8,128)S(1)} collective-permute-done((f32[128,128]{1,0:T(8,128)S(1)}, f32[128,128]{1,0:T(8,128)S(1)}, u32[]{:S(2)}, u32[]{:S(2)}) %collective-permute-start.19) | collective-permute-done | bytes 65568 | tf_op jit(solution)/shard_map/ppermute | solution.py:271
  153.9 5.6 %collective-permute-start.21 = (f32[128,128]{1,0:T(8,128)S(1)}, f32[128,128]{1,0:T(8,128)S(1)}, u32[]{:S(2)}, u32[]{:S(2)}) collective-permute-start(f32[128,128]{1,0:T(8,128)S(1)} %add_add_fusion.1.sa_ref), channel_id=1, source_target_pairs={{0,1},{1,0},{2,3},{3,2},{4,5},{5,4},{6,7},{7,6},{8,9},{9,8},{10,11... | collective-permute-start | bytes 196616 | tf_op jit(solution)/shard_map/ppermute | solution.py:319
  159.5 4.6 %coupling.1.t_ref = f32[128,128]{1,0:T(8,128)S(1)} custom-call(f32[128,128]{1,0:T(8,128)S(1)} %get-tuple-element.11.h_ref), custom_call_target="tpu_custom_call" | custom-call | tf_op jit(solution)/shard_map/coupling/pallas_call | solution.py:169
  164.1 2.8 %left.1 = (bf16[1024,256]{1,0:T(8,128)(2,1)S(1)}, bf16[1024,256]{1,0:T(8,128)(2,1)S(1)}) custom-call(s32[1]{0:T(128)} %bitcast.place_ref, f32[1024,128]{1,0:T(8,128)S(1)} %copy-done.1, f32[1024,128]{1,0:T(8,128)S(1)} %bitcast.26, f32[128,128]{1,0:T(8,128)S(1)} %get-tuple-element.9.r_ref, f32[128,128]{1,0:T(8,128)S(1)} %coupling.1.t_ref, ...), custom_call_target="tpu_custom_call" | custom-call | tf_op jit(solution)/shard_map/left/pallas_call | solution.py:216
  168.5 1.0 copy-done.3
  170.6 10.6 %update.1 = f32[1024,2048]{1,0:T(8,128)} custom-call(f32[1024,2048]{1,0:T(8,128)} %a_ref.3, bf16[1024,256]{1,0:T(8,128)(2,1)S(1)} %copy-done.3, bf16[1024,256]{1,0:T(8,128)(2,1)S(1)} %copy-done.5, f32[2048,256]{1,0:T(8,128)S(1)} %bitcast.25), custom_call_target="tpu_custom_call" | custom-call | flops 3221225472 | bytes 16777216 | tf_op jit(solution)/shard_map/update/pallas_call | solution.py:237
  (50 shorter events, 9.6 us)
Async XLA Ops:
  0.6 1.0 copy-start
  1.7 22.9 %copy-start.1 = (f32[1024,128]{1,0:T(8,128)S(1)}, f32[1024,128]{1,0:T(8,128)}, u32[]{:S(2)}) copy-start(f32[1024,128]{1,0:T(8,128)} %p_ref.5) | copy-start | bytes 1572868
  2.3 27.8 %collective-permute-start.7 = (f32[128,256]{1,0:T(8,128)S(1)}, f32[128,256]{1,0:T(8,128)S(1)}, u32[]{:S(2)}, u32[]{:S(2)}) collective-permute-start(f32[128,256]{1,0:T(8,128)S(1)} %gram.1), channel_id=1, source_target_pairs={{0,24},{8,0},{16,8},{24,16},{32,56},{40,32},{48,40},{56,48},{64,88... | collective-permute-start | bytes 393224 | tf_op jit(solution)/shard_map/ppermute | solution.py:271
  5.7 25.8 %collective-permute-start.6 = (f32[128,256]{1,0:T(8,128)S(1)}, f32[128,256]{1,0:T(8,128)S(1)}, u32[]{:S(2)}, u32[]{:S(2)}) collective-permute-start(f32[128,256]{1,0:T(8,128)S(1)} %gram.1), channel_id=1, source_target_pairs={{0,8},{8,16},{16,24},{24,0},{32,40},{40,48},{48,56},{56,32},{64,72... | collective-permute-start | bytes 393224 | tf_op jit(solution)/shard_map/ppermute | solution.py:271
  5.7 25.8 %collective-permute-start.5 = (f32[128,256]{1,0:T(8,128)S(1)}, f32[128,256]{1,0:T(8,128)S(1)}, u32[]{:S(2)}, u32[]{:S(2)}) collective-permute-start(f32[128,256]{1,0:T(8,128)S(1)} %gram.1), channel_id=1, source_target_pairs={{0,16},{8,24},{16,0},{24,8},{32,48},{40,56},{48,32},{56,40},{64,80... | collective-permute-start | bytes 393224 | tf_op jit(solution)/shard_map/ppermute | solution.py:271
  8.5 16.0 %collective-permute-start = (f32[4,128,128]{2,1,0:T(8,128)S(1)}, f32[4,128,128]{2,1,0:T(8,128)S(1)}, u32[]{:S(2)}, u32[]{:S(2)}) collective-permute-start(f32[4,128,128]{2,1,0:T(8,128)S(1)} %slice_bitcast_fusion), channel_id=1, source_target_pairs={{0,1},{8,9},{16,17},{24,25},{32,33},{40,41},{48,49},{56,57},{64,65... | collective-permute-start | bytes 786440 | tf_op jit(solution)/shard_map/ppermute | solution.py:300
  18.2 56.0 %all-to-all-start = ((f32[16,128,128]{2,1,0:T(8,128)}), f32[16,128,128]{2,1,0:T(8,128)S(1)}, u32[]{:S(2)}, u32[]{:S(2)}) async-start(f32[16,128,128]{2,1,0:T(8,128)} %product.1), calls=%async_computation | async-start | bytes 2097152 | tf_op jit(solution)/shard_map/all_to_all | solution.py:297
  24.6 10.1 %collective-permute-start.2 = (f32[128,128]{1,0:T(8,128)S(1)}, f32[128,128]{1,0:T(8,128)S(1)}, u32[]{:S(2)}, u32[]{:S(2)}) collective-permute-start(f32[128,128]{1,0:T(8,128)S(1)} %get-tuple-element.16), channel_id=1, source_target_pairs={{0,4},{1,5},{8,12},{9,13},{16,20},{17,21},{24,28},{25,29},{32,36},... | collective-permute-start | bytes 196616 | tf_op jit(solution)/shard_map/ppermute | solution.py:301
  28.8 6.5 %collective-permute-start.3 = (f32[128,128]{1,0:T(8,128)S(1)}, f32[128,128]{1,0:T(8,128)S(1)}, u32[]{:S(2)}, u32[]{:S(2)}) collective-permute-start(f32[128,128]{1,0:T(8,128)S(1)} %get-tuple-element.17), channel_id=1, source_target_pairs={{0,6},{1,7},{8,14},{9,15},{16,22},{17,23},{24,30},{25,31},{32,38},... | collective-permute-start | bytes 196616 | tf_op jit(solution)/shard_map/ppermute | solution.py:301
  30.2 5.2 %collective-permute-start.1 = (f32[128,128]{1,0:T(8,128)S(1)}, f32[128,128]{1,0:T(8,128)S(1)}, u32[]{:S(2)}, u32[]{:S(2)}) collective-permute-start(f32[128,128]{1,0:T(8,128)S(1)} %get-tuple-element.18), channel_id=1, source_target_pairs={{0,2},{1,3},{8,10},{9,11},{16,18},{17,19},{24,26},{25,27},{32,34},... | collective-permute-start | bytes 196616 | tf_op jit(solution)/shard_map/ppermute | solution.py:301
  31.5 10.3 %collective-permute-start.10 = (f32[128,256]{1,0:T(8,128)S(1)}, f32[128,256]{1,0:T(8,128)S(1)}, u32[]{:S(2)}, u32[]{:S(2)}) collective-permute-start(f32[128,256]{1,0:T(8,128)S(1)} %add_add_fusion.a_ref), channel_id=1, source_target_pairs={{0,96},{8,104},{16,112},{24,120},{32,0},{40,8},{48,16},{56,24},{64... | collective-permute-start | bytes 393224 | tf_op jit(solution)/shard_map/ppermute | solution.py:271
  34.2 7.6 %collective-permute-start.9 = (f32[128,256]{1,0:T(8,128)S(1)}, f32[128,256]{1,0:T(8,128)S(1)}, u32[]{:S(2)}, u32[]{:S(2)}) collective-permute-start(f32[128,256]{1,0:T(8,128)S(1)} %add_add_fusion.a_ref), channel_id=1, source_target_pairs={{0,64},{8,72},{16,80},{24,88},{32,96},{40,104},{48,112},{56,120},{... | collective-permute-start | bytes 393224 | tf_op jit(solution)/shard_map/ppermute | solution.py:271
  34.7 11.5 %collective-permute-start.8 = (f32[128,256]{1,0:T(8,128)S(1)}, f32[128,256]{1,0:T(8,128)S(1)}, u32[]{:S(2)}, u32[]{:S(2)}) collective-permute-start(f32[128,256]{1,0:T(8,128)S(1)} %add_add_fusion.a_ref), channel_id=1, source_target_pairs={{0,32},{8,40},{16,48},{24,56},{32,64},{40,72},{48,80},{56,88},{64,... | collective-permute-start | bytes 393224 | tf_op jit(solution)/shard_map/ppermute | solution.py:271
  35.4 38.8 %collective-permute-start.4 = (f32[128,256]{1,0:T(8,128)S(1)}, f32[128,256]{1,0:T(8,128)S(1)}, u32[]{:S(2)}, u32[]{:S(2)}) collective-permute-start(f32[128,256]{1,0:T(8,128)S(1)} %pad_maximum_fusion), channel_id=1, source_target_pairs={{0,0},{1,8},{2,16},{3,24},{4,32},{5,40},{6,48},{7,56},{8,64},{9,72... | collective-permute-start | bytes 393224 | tf_op jit(solution)/shard_map/ppermute | solution.py:304
  74.8 5.6 %collective-permute-start.11 = (f32[128,128]{1,0:T(8,128)S(1)}, f32[128,128]{1,0:T(8,128)S(1)}, u32[]{:S(2)}, u32[]{:S(2)}) collective-permute-start(f32[128,128]{1,0:T(8,128)S(1)} %slice.31), channel_id=1, source_target_pairs={{0,0},{8,1},{16,2},{24,3},{32,4},{40,5},{48,6},{56,7},{64,8},{72,9... | collective-permute-start | bytes 196616 | tf_op jit(solution)/shard_map/ppermute | solution.py:311
  101.6 66.8 %all-to-all-start.2 = ((f32[16,128,256]{2,1,0:T(8,128)}), f32[16,128,256]{2,1,0:T(8,128)S(1)}, u32[]{:S(2)}, u32[]{:S(2)}) async-start(f32[16,128,256]{2,1,0:T(8,128)} %broadcast_in_dim.7), calls=%async_computation.2 | async-start | bytes 4194304 | tf_op jit(solution)/shard_map/all_to_all | solution.py:310
  109.8 27.7 %collective-permute-start.14 = (f32[128,128]{1,0:T(8,128)S(1)}, f32[128,128]{1,0:T(8,128)S(1)}, u32[]{:S(2)}, u32[]{:S(2)}) collective-permute-start(f32[128,128]{1,0:T(8,128)S(1)} %get-tuple-element.12), channel_id=1, source_target_pairs={{0,24},{8,0},{16,8},{24,16},{32,56},{40,32},{48,40},{56,48},{64,88... | collective-permute-start | bytes 196616 | tf_op jit(solution)/shard_map/ppermute | solution.py:271
  112.4 25.6 %collective-permute-start.13 = (f32[128,128]{1,0:T(8,128)S(1)}, f32[128,128]{1,0:T(8,128)S(1)}, u32[]{:S(2)}, u32[]{:S(2)}) collective-permute-start(f32[128,128]{1,0:T(8,128)S(1)} %get-tuple-element.12), channel_id=1, source_target_pairs={{0,8},{8,16},{16,24},{24,0},{32,40},{40,48},{48,56},{56,32},{64,72... | collective-permute-start | bytes 196616 | tf_op jit(solution)/shard_map/ppermute | solution.py:271
  112.4 28.4 %collective-permute-start.12 = (f32[128,128]{1,0:T(8,128)S(1)}, f32[128,128]{1,0:T(8,128)S(1)}, u32[]{:S(2)}, u32[]{:S(2)}) collective-permute-start(f32[128,128]{1,0:T(8,128)S(1)} %get-tuple-element.12), channel_id=1, source_target_pairs={{0,16},{8,24},{16,0},{24,8},{32,48},{40,56},{48,32},{56,40},{64,80... | collective-permute-start | bytes 196616 | tf_op jit(solution)/shard_map/ppermute | solution.py:271
  140.9 4.1 %collective-permute-start.17 = (f32[128,128]{1,0:T(8,128)S(1)}, f32[128,128]{1,0:T(8,128)S(1)}, u32[]{:S(2)}, u32[]{:S(2)}) collective-permute-start(f32[128,128]{1,0:T(8,128)S(1)} %add_add_fusion.3), channel_id=1, source_target_pairs={{0,96},{8,104},{16,112},{24,120},{32,0},{40,8},{48,16},{56,24},{64... | collective-permute-start | bytes 196616 | tf_op jit(solution)/shard_map/ppermute | solution.py:271
  142.7 5.0 %collective-permute-start.16 = (f32[128,128]{1,0:T(8,128)S(1)}, f32[128,128]{1,0:T(8,128)S(1)}, u32[]{:S(2)}, u32[]{:S(2)}) collective-permute-start(f32[128,128]{1,0:T(8,128)S(1)} %add_add_fusion.3), channel_id=1, source_target_pairs={{0,32},{8,40},{16,48},{24,56},{32,64},{40,72},{48,80},{56,88},{64,... | collective-permute-start | bytes 196616 | tf_op jit(solution)/shard_map/ppermute | solution.py:271
  142.7 5.0 %collective-permute-start.15 = (f32[128,128]{1,0:T(8,128)S(1)}, f32[128,128]{1,0:T(8,128)S(1)}, u32[]{:S(2)}, u32[]{:S(2)}) collective-permute-start(f32[128,128]{1,0:T(8,128)S(1)} %add_add_fusion.3), channel_id=1, source_target_pairs={{0,64},{8,72},{16,80},{24,88},{32,96},{40,104},{48,112},{56,120},{... | collective-permute-start | bytes 196616 | tf_op jit(solution)/shard_map/ppermute | solution.py:271
  147.8 3.4 %collective-permute-start.20 = (f32[128,128]{1,0:T(8,128)S(1)}, f32[128,128]{1,0:T(8,128)S(1)}, u32[]{:S(2)}, u32[]{:S(2)}) collective-permute-start(f32[128,128]{1,0:T(8,128)S(1)} %add_add_fusion.2), channel_id=1, source_target_pairs={{0,6},{1,7},{2,0},{3,1},{4,2},{5,3},{6,4},{7,5},{8,14},{9,15},{10,... | collective-permute-start | bytes 196616 | tf_op jit(solution)/shard_map/ppermute | solution.py:271
  148.7 4.3 %collective-permute-start.19 = (f32[128,128]{1,0:T(8,128)S(1)}, f32[128,128]{1,0:T(8,128)S(1)}, u32[]{:S(2)}, u32[]{:S(2)}) collective-permute-start(f32[128,128]{1,0:T(8,128)S(1)} %add_add_fusion.2), channel_id=1, source_target_pairs={{0,2},{1,3},{2,4},{3,5},{4,6},{5,7},{6,0},{7,1},{8,10},{9,11},{10,... | collective-permute-start | bytes 196616 | tf_op jit(solution)/shard_map/ppermute | solution.py:271
  149.3 4.6 %collective-permute-start.18 = (f32[128,128]{1,0:T(8,128)S(1)}, f32[128,128]{1,0:T(8,128)S(1)}, u32[]{:S(2)}, u32[]{:S(2)}) collective-permute-start(f32[128,128]{1,0:T(8,128)S(1)} %add_add_fusion.2), channel_id=1, source_target_pairs={{0,4},{1,5},{2,6},{3,7},{4,0},{5,1},{6,2},{7,3},{8,12},{9,13},{10,... | collective-permute-start | bytes 196616 | tf_op jit(solution)/shard_map/ppermute | solution.py:271
  153.9 10.2 %collective-permute-start.21 = (f32[128,128]{1,0:T(8,128)S(1)}, f32[128,128]{1,0:T(8,128)S(1)}, u32[]{:S(2)}, u32[]{:S(2)}) collective-permute-start(f32[128,128]{1,0:T(8,128)S(1)} %add_add_fusion.1.sa_ref), channel_id=1, source_target_pairs={{0,1},{1,0},{2,3},{3,2},{4,5},{5,4},{6,7},{7,6},{8,9},{9,8},{10,11... | collective-permute-start | bytes 196616 | tf_op jit(solution)/shard_map/ppermute | solution.py:319
  166.9 0.8 copy-start.2
  167.7 0.8 copy-start.4
  168.5 1.0 copy-start.3
  169.5 1.0 copy-start.5

commit v2 on v1

v2 whole, which is shorter than its diff:
```python
import jax
import jax.numpy as jnp
from jax import lax
from jax.experimental import pallas as pl
from jax.experimental.pallas import tpu as pltpu
from jax.sharding import PartitionSpec as P

B = 128
ZN, XN, YN, CN = 4, 4, 4, 2
F32, BF16 = jnp.float32, jnp.bfloat16
VMEM_LIMIT = 48 * 1024 * 1024


def hdot(left, right, dims=((1,), (0,))):
    return lax.dot_general(
        left, right, (dims, ((), ())), precision=lax.Precision.HIGHEST, preferred_element_type=F32
    )


def bdot(left, right, dims=((1,), (0,))):
    return lax.dot_general(left, right, (dims, ((), ())), preferred_element_type=F32)


def split(value):
    high = value.astype(BF16)
    return high, (value - high.astype(F32)).astype(BF16)


def dot3(left, right, dims=((1,), (0,))):
    (lh, ll), (rh, rl) = split(left), split(right)
    return bdot(lh, rh, dims) + (bdot(lh, rl, dims) + bdot(ll, rh, dims))


def iotas(shape=(B, B)):
    return lax.broadcasted_iota(jnp.int32, shape, 0), lax.broadcasted_iota(jnp.int32, shape, 1)


def eye():
    r, c = iotas()
    return jnp.where(r == c, 1.0, 0.0).astype(F32)


def params(**kw):
    return pltpu.CompilerParams(vmem_limit_bytes=VMEM_LIMIT, **kw)


STEPS = 6


def inverse_factor(gram, out_ref, s_ref, x_ref):
    r, c = iotas()
    one = eye()
    diag_row = jnp.sum(one * gram, axis=0, keepdims=True)
    diag_col = jnp.sum(one * gram, axis=1, keepdims=True)
    scale_row, scale_col = lax.rsqrt(diag_row), lax.rsqrt(diag_col)
    corr = gram * scale_row * scale_col
    x = one
    err = corr - one
    for step in range(STEPS):
        if step:
            err = hdot(hdot(x, corr), x, ((1,), (1,))) - one
        phi = jnp.where(r > c, err, jnp.where(r == c, 0.5 * err, 0.0))
        x = x - (phi if step == 0 else hdot(phi, x))
    out_ref[...] = x * scale_row
    size = jnp.sum(err * err)
    good = size < 1e-8

    @pl.when(jnp.logical_not(good))
    def _():
        s_ref[...] = corr
        x_ref[...] = one

        def body(k, carry):
            row = s_ref[pl.ds(k, 1), :]
            rr, cc = iotas()
            ident = rr == cc
            lane = lax.broadcasted_iota(jnp.int32, (1, B), 1)
            pivot = jnp.sum(jnp.where(lane == k, row, 0.0), axis=1, keepdims=True)
            inv = lax.rsqrt(pivot)
            row = row * inv
            col = jnp.sum(jnp.where(ident, jnp.broadcast_to(row, (B, B)), 0.0), axis=1, keepdims=True)
            below = lax.broadcasted_iota(jnp.int32, (B, 1), 0) > k
            col = jnp.where(below, col, 0.0)
            xrow = x_ref[pl.ds(k, 1), :] * inv
            x_ref[pl.ds(k, 1), :] = xrow
            s_ref[...] = s_ref[...] - col * row
            x_ref[...] = x_ref[...] - col * xrow
            return carry

        lax.fori_loop(0, B, body, 0)
        out_ref[...] = x_ref[...] * scale_row


SMEM = pl.BlockSpec(memory_space=pltpu.SMEM)
VMEM = pl.BlockSpec(memory_space=pltpu.VMEM)


def shaped(*shape, dtype=F32):
    return jax.ShapeDtypeStruct(shape, dtype)


ANY = pl.BlockSpec(memory_space=pl.ANY)


def gram_kernel(panel):
    def body(p_ref, out_ref):
        p = p_ref[...]
        out_ref[...] = hdot(p, p, ((0,), (0,)))

    return pl.pallas_call(body, out_shape=shaped(B, B), compiler_params=params(), name="gram")(panel)


def product_kernel(panel, rinv, trailing, first_row, after):
    rows, cols = trailing.shape
    tile = 1024
    chunks = tile // B

    def body(first_ref, p_ref, r_ref, a_ref, *refs):
        v_ref, out_ref, vh_ref = refs[-3:]

        @pl.when(pl.program_id(0) == 0)
        def _():
            r, c = iotas((rows, B))
            v = dot3(p_ref[...], r_ref[...]) + jnp.where((r == c) & (first_ref[0] == 1), 1.0, 0.0)
            v_ref[...] = v
            vh_ref[:B], vh_ref[B:] = split(v.T)

        ah, al = split(a_ref[...])
        both = bdot(vh_ref[...], ah)
        z = both[:B] + (both[B:] + bdot(vh_ref[:B], al))
        for k in range(chunks):
            out_ref[k, 0] = z[:, k * B : (k + 1) * B]

    return pl.pallas_call(
        body,
        grid=(cols // tile,),
        out_shape=(shaped(rows, B), shaped(chunks, cols // tile, B, B)),
        in_specs=[
            SMEM,
            pl.BlockSpec((rows, B), lambda t: (0, 0)),
            pl.BlockSpec((B, B), lambda t: (0, 0)),
            pl.BlockSpec((rows, tile), lambda t: (0, t)),
        ]
        + [ANY] * len(after),
        out_specs=(
            pl.BlockSpec((rows, B), lambda t: (0, 0)),
            pl.BlockSpec((chunks, 1, B, B), lambda t: (0, t, 0, 0)),
        ),
        scratch_shapes=[pltpu.VMEM((2 * B, rows), BF16)],
        compiler_params=params(),
        cost_estimate=pl.CostEstimate(flops=6 * rows * cols * B, bytes_accessed=4 * rows * cols, transcendentals=0),
        name="product",
    )(first_row, panel, rinv, trailing, *after)


def factor_kernel(parts):
    def body(a_ref, b_ref, c_ref, d_ref, band_ref, rinv_ref, linv_ref, s_ref, x_ref):
        gram = (a_ref[...] + c_ref[...]) + (b_ref[...] + d_ref[...])
        inverse_factor(gram, linv_ref, s_ref, x_ref)
        linv = linv_ref[...]
        rinv_ref[...] = linv.T
        r, c = iotas()
        band_ref[...] = jnp.where(r <= c, -hdot(linv, gram), -0.0)

    square = shaped(B, B)
    return pl.pallas_call(
        body,
        out_shape=(square, square),
        scratch_shapes=[pltpu.VMEM((B, B), F32)] * 3,
        compiler_params=params(),
        name="factor",
    )(*parts)


def chunk_kernel(pieces, after):
    count = pieces.shape[0]

    def body(y_ref, after_ref, w_ref):
        total = [y_ref[k] for k in range(count)]
        while len(total) > 1:
            total = [l + r for l, r in zip(total[::2], total[1::2])]
        w_ref[...] = total[0].T

    return pl.pallas_call(
        body, out_shape=shaped(B, B), in_specs=[VMEM, ANY], compiler_params=params(), name="chunk"
    )(pieces, after)


def copies_kernel(w, v, count, after):
    def body(w_ref, v_ref, after_ref, copies_ref):
        for k in range(count):
            copies_ref[k, :, :B] = w_ref[...]
            copies_ref[k, :, B:] = v_ref[...]

    return pl.pallas_call(
        body, out_shape=shaped(count, B, 2 * B), in_specs=[VMEM, VMEM, ANY], compiler_params=params(), name="copies"
    )(w, v, after)


def small_kernel(right, after):
    rows = right.shape[0] * right.shape[1] * B

    def body(r_ref, after_ref, out_ref):
        both = r_ref[...].reshape(rows, 2 * B)
        out_ref[...] = dot3(both[:, B:], both[:, :B], ((0,), (0,)))

    return pl.pallas_call(
        body, out_shape=shaped(B, B), in_specs=[VMEM, ANY], compiler_params=params(), name="small"
    )(right, after)


def mixed_kernel(w_parts, coupling, place):
    part = w_parts[0].shape[0]

    def body(place_ref, t_ref, *refs):
        part_refs, out_ref = refs[:YN], refs[YN]
        for d in range(YN):
            y = lax.rem(place_ref[1] + (YN - d), YN)
            out_ref[pl.ds(pl.multiple_of(y * part, part), part), :] = dot3(part_refs[d][...], t_ref[...])

    return pl.pallas_call(
        body,
        out_shape=shaped(YN * part, B),
        in_specs=[SMEM] + [VMEM] * (YN + 1),
        compiler_params=params(),
        name="mixed",
    )(place, coupling, *w_parts)


def coupling_kernel(tops, rinv):
    def body(*refs):
        top_refs, (r_ref, out_ref, linv_ref, s_ref, x_ref) = refs[:4], refs[4:]
        top = (top_refs[0][...] + top_refs[1][...]) + (top_refs[2][...] + top_refs[3][...])
        m = eye() + hdot(top, r_ref[...]).T
        inverse_factor(hdot(m, m, ((0,), (0,))), linv_ref, s_ref, x_ref)
        linv = linv_ref[...]
        out_ref[...] = hdot(linv, hdot(linv, m, ((1,), (1,))), ((0,), (0,)))

    return pl.pallas_call(
        body,
        out_shape=shaped(B, B),
        scratch_shapes=[pltpu.VMEM((B, B), F32)] * 3,
        compiler_params=params(),
        name="coupling",
    )(*tops, rinv)


def turned_kernel(v, coupling):
    def body(v_ref, t_ref, h_ref, l_ref):
        h_ref[...], l_ref[...] = split(dot3(v_ref[...], t_ref[...], ((1,), (1,))))

    half = shaped(*v.shape, dtype=BF16)
    return pl.pallas_call(body, out_shape=(half, half), compiler_params=params(), name="turned")(v, coupling)


def update_kernel(trailing, right, v, turned, mixed, coupling, parts):
    rows, cols = trailing.shape
    tile = 512
    chunks = tile // B

    def body(a_ref, right_ref, v_ref, th_ref, tl_ref, m_ref, t_ref, *refs):
        s_refs, (out_ref, h_ref, l_ref) = refs[:YN], refs[YN:]

        @pl.when(pl.program_id(0) == 0)
        def _():
            t = t_ref[...]
            s = [ref[...] for ref in s_refs]
            small = hdot(hdot(t, (s[0] + s[2]) + (s[1] + s[3]), ((0,), (0,))), t)
            small = 0.5 * (small + small.T)
            h_ref[:, :B], l_ref[:, :B] = th_ref[...], tl_ref[...]
            h_ref[:, B:], l_ref[:, B:] = split(m_ref[...] - dot3(v_ref[...], small))

        rh, rl = split(right_ref[...].reshape(tile, 2 * B))
        h = h_ref[...]
        nt = ((1,), (1,))
        out_ref[...] = a_ref[...] - (bdot(h, rh, nt) + (bdot(h, rl, nt) + bdot(l_ref[...], rh, nt)))

    def whole(*shape):
        return pl.BlockSpec(shape, lambda t: (0, 0))

    per_half = right.shape[0] // chunks
    return pl.pallas_call(
        body,
        grid=(cols // tile,),
        out_shape=shaped(rows, cols),
        in_specs=[
            pl.BlockSpec((rows, tile), lambda t: (0, t)),
            pl.BlockSpec((chunks, 1, B, 2 * B), lambda t: (t % per_half, t // per_half, 0, 0)),
            whole(rows, B),
            whole(rows, B),
            whole(rows, B),
            whole(rows, B),
            whole(B, B),
        ]
        + [whole(B, B)] * YN,
        out_specs=pl.BlockSpec((rows, tile), lambda t: (0, t)),
        scratch_shapes=[pltpu.VMEM((rows, 2 * B), BF16)] * 2,
        compiler_params=params(),
        cost_estimate=pl.CostEstimate(flops=12 * rows * cols * B, bytes_accessed=8 * rows * cols, transcendentals=0),
        name="update",
    )(trailing, right, v, *turned, mixed, coupling, *parts)


def along_x(d):
    return [(z * XN + x, z * XN + (x + d) % XN) for z in range(ZN) for x in range(XN)]


def along_z(d):
    return [(z * XN + x, (z + d) % ZN * XN + x) for z in range(ZN) for x in range(XN)]


def along_y(d):
    return [(y * CN + c, (y + d) % YN * CN + c) for y in range(YN) for c in range(CN)]


def along_c(d):
    return [(y * CN + c, y * CN + (c + d) % CN) for y in range(YN) for c in range(CN)]


def four(value, axis, along):
    return [value] + [lax.ppermute(value, axis, along(d)) for d in (1, 2, 3)]


def add_four(parts):
    return (parts[0] + parts[2]) + (parts[1] + parts[3])


def to_all(copies, axis):
    return lax.all_to_all(copies, axis, split_axis=0, concat_axis=0, tiled=True)


def shards(panel, trailing):
    rows, cols = trailing.shape
    prow = lax.axis_size("prow")
    i, j = lax.axis_index("prow"), lax.axis_index("pcol")
    y, c, x = j // CN, j % CN, i % XN
    place = jnp.stack([i, y]).astype(jnp.int32)
    first_row = (i == 0).astype(jnp.int32).reshape(1)

    def device(z, x, y, c):
        return ((z * XN + x) * YN + y) * CN + c

    coords = [(z, x, y, c) for z in range(ZN) for x in range(XN) for y in range(YN) for c in range(CN)]
    swap = [(device(y, 2 * c + x % 2, z, x // 2), device(z, x, y, c)) for z, x, y, c in coords]

    top = jnp.where(i == 0, panel[:B], jnp.zeros_like(panel[:B]))
    parts = four(gram_kernel(panel), "prow", along_x)
    top = top + sum(lax.ppermute(top, "prow", [(0, k)]) for k in range(1, XN))
    parts = four(add_four(parts), "prow", along_z)
    tops = [top] + [lax.ppermute(top, "prow", [(k, z * XN + k) for k in range(XN)]) for z in range(1, ZN)]
    band, rinv = factor_kernel(parts)
    v, chunks = product_kernel(panel, rinv, trailing, first_row, tops)
    pieces = to_all(chunks.reshape(prow, B, B), "prow")

    v_chunk = lax.ppermute(lax.dynamic_slice_in_dim(v, j * B, B, 0), ("prow", "pcol"), swap)
    tops[0], _ = lax.optimization_barrier((tops[0], v))
    coupling = coupling_kernel(tops, rinv)
    turned = turned_kernel(v, coupling)

    w = chunk_kernel(pieces, turned[0])
    row_w = lax.ppermute(w, ("prow", "pcol"), swap)
    right = to_all(copies_kernel(w, v_chunk, prow, row_w), "prow").reshape(*chunks.shape[:3], 2 * B)

    other = lax.ppermute(row_w, "pcol", along_c(1))
    row_w = jnp.concatenate([jnp.where(c == 0, row_w, other), jnp.where(c == 0, other, row_w)])
    mixed = mixed_kernel(four(row_w, "pcol", along_y), coupling, place)

    part = small_kernel(right, mixed)
    part = part + lax.ppermute(part, "pcol", along_c(1))
    parts = four(part, "pcol", along_y)
    return update_kernel(trailing, right, v, turned, mixed, coupling, parts), band


def solution(mesh):
    placed = (P("prow", None), P("prow", "pcol"))
    return jax.shard_map(
        shards, mesh=mesh, in_specs=placed, out_specs=(P("prow", "pcol"), P()), check_vma=False
    )
```

time: 182 us -> 148 us (0.81)
  blocking collectives: 19.7 us -> 0 us
  waiting for transfers between devices: 38.2 us -> 19.9 us
  Pallas kernels: 55.5 us -> 51.2 us
  local copies, waits for them, and re-layouts: 7.39 us -> 10.6 us
  starting transfers between devices: 59.4 us -> 62.5 us
    ppermute x15 -> x12, waiting for transfers between devices: 36.9 us -> 10.7 us  [four(): return [value] + [lax.ppermute(value, axis, along(d)) for d in (1, 2, 3)]]
    all_to_all x1 -> x0, blocking collectives: 19.7 us -> none  [shards(): lax.all_to_all(copies, 'pcol', split_axis=0, concat_axis=0, tiled=True)]
    ppermute x7 -> x10, starting transfers between devices: 24.1 us -> 35 us  [the longest x1 7.64 us: shards(): lax.ppermute(lax.dynamic_slice_in_dim(v, j * B, B, 0), ('prow', 'pcol'),...]
    ppermute x15 -> x12, starting transfers between devices: 20.8 us -> 14.4 us  [four(): return [value] + [lax.ppermute(value, axis, along(d)) for d in (1, 2, 3)]]
    unnamed x12 -> x26, local copies, waits for them, and re-layouts: 4.71 us -> 10.6 us
    all_to_all x2, waiting for transfers between devices: 0.01 us -> 5.48 us  [to_all(): return lax.all_to_all(copies, axis, split_axis=0, concat_axis=0, tiled=True)]
    pallas_call x7 -> x10, Pallas kernels: 55.5 us -> 51.2 us  [the longest x1 27.9 us: factor_kernel(): pl.pallas_call(body, out_shape=(square, square), scratch_shapes=[pltpu.VM...]
    ppermute x7 -> x10, waiting for transfers between devices: 1.35 us -> 3.75 us  [the longest x1 1.92 us: shards(): row_w = lax.ppermute(w, ('prow', 'pcol'), swap)]
  transfers between devices with their start and end apart: 24 -> 24, of which waited for: 9 -> 10; matrix products, arithmetic and copies ran while one was open for 1% -> 1% of each run, Pallas kernels for 24% -> 23%
where the time goes in v2:
time: 148 us; the launch traced here: 147 us
  starting transfers between devices  62.5 us (42%)
  Pallas kernels  51.2 us (35%)
  waiting for transfers between devices  19.9 us (13%)
  local copies, waits for them, and re-layouts  10.6 us (7%)
  other arithmetic  1.83 us (1%)
    pallas_call x1, Pallas kernels, factor_kernel(): pl.pallas_call(body, out_shape=(square, square), scratch_shapes=[pltpu.VM...  27.9 us
    ppermute x12, starting transfers between devices, four(): return [value] + [lax.ppermute(value, axis, along(d)) for d in (1, 2, 3)]  14.4 us
    all_to_all x2, starting transfers between devices, to_all(): return lax.all_to_all(copies, axis, split_axis=0, concat_axis=0, tiled=True)  13.2 us
    ppermute x12, waiting for transfers between devices, four(): return [value] + [lax.ppermute(value, axis, along(d)) for d in (1, 2, 3)]  10.7 us
    unnamed x26, local copies, waits for them, and re-layouts  10.6 us
    pallas_call x1, Pallas kernels, update_kernel(): pl.pallas_call(body, grid=(cols // tile,), out_shape=shaped(rows, cols),...  10.1 us
    ppermute x1, starting transfers between devices, shards(): lax.ppermute(lax.dynamic_slice_in_dim(v, j * B, B, 0), ('prow', 'pcol'),...  7.64 us
    ppermute x3, starting transfers between devices, shards(): lax.ppermute(top, 'prow', [(k, z * XN + k) for k in range(XN)])  7.37 us
  transfers between devices with their start and end apart: 24, of which 10 were waited for; matrix products, arithmetic and copies ran while one was open for 1% of the time, Pallas kernels for 23%

profile of v2, /device:TPU:1, one launch (start us, length us, event | category | flops | bytes accessed | tf_op | source)
XLA Modules:
  0.0 147.0 jit_solution(6754971020408011089)
XLA Ops:
  0.6 1.0 copy-done.1
  2.3 3.4 %collective-permute-start.2 = (f32[128,128]{1,0:T(8,128)S(1)}, f32[128,128]{1,0:T(8,128)S(1)}, u32[]{:S(2)}, u32[]{:S(2)}) collective-permute-start(f32[128,128]{1,0:T(8,128)S(1)} %gram.1), channel_id=1, source_target_pairs={{0,24},{8,0},{16,8},{24,16},{32,56},{40,32},{48,40},{56,48},{64,88... | collective-permute-start | bytes 196616 | tf_op jit(solution)/shard_map/ppermute | solution.py:321
  5.7 1.7 %collective-permute-start = (f32[128,128]{1,0:T(8,128)S(1)}, f32[128,128]{1,0:T(8,128)S(1)}, u32[]{:S(2)}, u32[]{:S(2)}) collective-permute-start(f32[128,128]{1,0:T(8,128)S(1)} %gram.1), channel_id=1, source_target_pairs={{0,16},{8,24},{16,0},{24,8},{32,48},{40,56},{48,32},{56,40},{64,80... | collective-permute-start | bytes 196616 | tf_op jit(solution)/shard_map/ppermute | solution.py:321
  8.3 2.8 %collective-permute-start.8 = (f32[128,128]{1,0:T(8,128)S(1)}, f32[128,128]{1,0:T(8,128)S(1)}, u32[]{:S(2)}, u32[]{:S(2)}) collective-permute-start(f32[128,128]{1,0:T(8,128)S(1)} %slice_select_fusion), channel_id=1, source_target_pairs={{0,24},{1,25},{2,26},{3,27},{4,28},{5,29},{6,30},{7,31}} | collective-permute-start | bytes 196616 | tf_op jit(solution)/shard_map/ppermute | solution.py:348
  11.1 1.3 collective-permute-start.7
  12.4 1.3 collective-permute-start.6
  16.3 4.2 %collective-permute-start.11 = (f32[128,128]{1,0:T(8,128)S(1)}, f32[128,128]{1,0:T(8,128)S(1)}, u32[]{:S(2)}, u32[]{:S(2)}) collective-permute-start(f32[128,128]{1,0:T(8,128)S(1)} %add_add_fusion.refs_0_), channel_id=1, source_target_pairs={{0,96},{8,104},{16,112},{24,120},{1,97},{9,105},{17,113},{25,121},... | collective-permute-start | bytes 196616 | tf_op jit(solution)/shard_map/ppermute | solution.py:350
  20.5 1.8 %collective-permute-start.10 = (f32[128,128]{1,0:T(8,128)S(1)}, f32[128,128]{1,0:T(8,128)S(1)}, u32[]{:S(2)}, u32[]{:S(2)}) collective-permute-start(f32[128,128]{1,0:T(8,128)S(1)} %add_add_fusion.refs_0_), channel_id=1, source_target_pairs={{0,64},{8,72},{16,80},{24,88},{1,65},{9,73},{17,81},{25,89},{2,66}... | collective-permute-start | bytes 196616 | tf_op jit(solution)/shard_map/ppermute | solution.py:350
  22.4 1.3 collective-permute-start.9
  23.7 27.9 %factor.1 = (f32[128,128]{1,0:T(8,128)}, f32[128,128]{1,0:T(8,128)S(1)}) custom-call(f32[128,128]{1,0:T(8,128)S(1)} %add_add_fusion.1.a_ref, f32[128,128]{1,0:T(8,128)S(1)} %collective-permute-done.3.b_ref, f32[128,128]{1,0:T(8,128)S(1)} %collective-permute-done.4.c_ref, f32[128,128]{1,0:T(8,128)S(1)} %collective-permute-done.5.d_ref), custom_call_target="tpu_custom_call" | custom-call | tf_op jit(solution)/shard_map/factor/pallas_call | solution.py:166
  51.6 1.0 copy-done.2
  52.6 5.6 %product.1 = (f32[1024,128]{1,0:T(8,128)S(1)}, f32[8,2,128,128]{3,2,1,0:T(8,128)}) custom-call(s32[1]{0:T(128)} %bitcast.first_ref, f32[1024,128]{1,0:T(8,128)S(1)} %copy-done.2, f32[128,128]{1,0:T(8,128)S(1)} %get-tuple-element.9.r_ref.refs_4_, f32[1024,2048]{1,0:T(8,128)} %a_ref.3, f32[128,128]{1,0:T(8,128)S(1)} %add_add_fusion.refs_0_, ...), custom_call_target="tpu_custom_call" | custom-call | flops 1610612736 | bytes 8388608 | tf_op jit(solution)/shard_map/product/pallas_call | solution.py:134
  58.3 3.7 %all-to-all-start = ((f32[16,128,128]{2,1,0:T(8,128)}), f32[16,128,128]{2,1,0:T(8,128)S(1)}, u32[]{:S(2)}, u32[]{:S(2)}) async-start(f32[16,128,128]{2,1,0:T(8,128)} %bitcast.1), calls=%async_computation | async-start | bytes 2097152 | tf_op jit(solution)/shard_map/all_to_all | solution.py:329
  61.9 7.6 %collective-permute-start.12 = (f32[128,128]{1,0:T(8,128)S(1)}, f32[128,128]{1,0:T(8,128)S(1)}, u32[]{:S(2)}, u32[]{:S(2)}) collective-permute-start(f32[128,128]{1,0:T(8,128)S(1)} %constant_dynamic-slice_fusion), channel_id=1, source_target_pairs={{0,0},{16,1},{32,2},{48,3},{64,4},{80,5},{96,6},{112,7},{8,8},{24,... | collective-permute-start | bytes 196616 | tf_op jit(solution)/shard_map/ppermute | solution.py:355
  69.6 4.8 %coupling.1.t_ref = f32[128,128]{1,0:T(8,128)S(1)} custom-call(f32[128,128]{1,0:T(8,128)S(1)} %add_add_fusion.refs_0_, f32[128,128]{1,0:T(8,128)S(1)} %collective-permute-done.9.refs_1_, f32[128,128]{1,0:T(8,128)S(1)} %collective-permute-done.10.refs_2_, f32[128,128]{1,0:T(8,128)S(1)} %collective-permute-done.11.refs_3_, ...), custom_call_target="tpu_custom_call" | custom-call | tf_op jit(solution)/shard_map/coupling/pallas_call | solution.py:239
  74.8 1.7 %all-to-all-done.y_ref = f32[16,128,128]{2,1,0:T(8,128)S(1)} async-done(((f32[16,128,128]{2,1,0:T(8,128)}), f32[16,128,128]{2,1,0:T(8,128)S(1)}, u32[]{:S(2)}, u32[]{:S(2)}) %all-to-all-start) | async-done | bytes 1048608 | tf_op jit(solution)/shard_map/all_to_all | solution.py:329
  76.6 5.8 %collective-permute-start.13 = (f32[128,128]{1,0:T(8,128)S(1)}, f32[128,128]{1,0:T(8,128)S(1)}, u32[]{:S(2)}, u32[]{:S(2)}) collective-permute-start(f32[128,128]{1,0:T(8,128)S(1)} %chunk.1.w_ref), channel_id=1, source_target_pairs={{0,0},{16,1},{32,2},{48,3},{64,4},{80,5},{96,6},{112,7},{8,8},{24,... | collective-permute-start | bytes 196616 | tf_op jit(solution)/shard_map/ppermute | solution.py:361
  82.4 1.9 %collective-permute-done.13.after_ref = f32[128,128]{1,0:T(8,128)S(1)} collective-permute-done((f32[128,128]{1,0:T(8,128)S(1)}, f32[128,128]{1,0:T(8,128)S(1)}, u32[]{:S(2)}, u32[]{:S(2)}) %collective-permute-start.13) | collective-permute-done | bytes 65568 | tf_op jit(solution)/shard_map/ppermute | solution.py:361
  84.5 1.3 copy-done
  85.8 9.5 %all-to-all-start.1 = ((f32[16,128,256]{2,1,0:T(8,128)}), f32[16,128,256]{2,1,0:T(8,128)S(1)}, u32[]{:S(2)}, u32[]{:S(2)}) async-start(f32[16,128,256]{2,1,0:T(8,128)} %copy-done), calls=%async_computation.1 | async-start | bytes 4194304 | tf_op jit(solution)/shard_map/all_to_all | solution.py:329
  95.4 3.0 %collective-permute-start.14 = (f32[128,128]{1,0:T(8,128)S(1)}, f32[128,128]{1,0:T(8,128)S(1)}, u32[]{:S(2)}, u32[]{:S(2)}) collective-permute-start(f32[128,128]{1,0:T(8,128)S(1)} %collective-permute-done.13.after_ref), channel_id=1, source_target_pairs={{0,1},{1,0},{2,3},{3,2},{4,5},{5,4},{6,7},{7,6},{8,9},{9,8},{10,11... | collective-permute-start | bytes 196616 | tf_op jit(solution)/shard_map/ppermute | solution.py:364
  99.3 2.7 %collective-permute-start.17 = (f32[256,128]{1,0:T(8,128)S(1)}, f32[256,128]{1,0:T(8,128)S(1)}, u32[]{:S(2)}, u32[]{:S(2)}) collective-permute-start(f32[256,128]{1,0:T(8,128)S(1)} %pad_maximum_fusion.refs_0_), channel_id=1, source_target_pairs={{0,6},{1,7},{2,0},{3,1},{4,2},{5,3},{6,4},{7,5},{8,14},{9,15},{10,... | collective-permute-start | bytes 393224 | tf_op jit(solution)/shard_map/ppermute | solution.py:321
  104.1 3.1 %collective-permute-done.17.refs_3_ = f32[256,128]{1,0:T(8,128)S(1)} collective-permute-done((f32[256,128]{1,0:T(8,128)S(1)}, f32[256,128]{1,0:T(8,128)S(1)}, u32[]{:S(2)}, u32[]{:S(2)}) %collective-permute-start.17) | collective-permute-done | bytes 131104 | tf_op jit(solution)/shard_map/ppermute | solution.py:321
  108.5 3.2 %collective-permute-done.15.refs_1_ = f32[256,128]{1,0:T(8,128)S(1)} collective-permute-done((f32[256,128]{1,0:T(8,128)S(1)}, f32[256,128]{1,0:T(8,128)S(1)}, u32[]{:S(2)}, u32[]{:S(2)}) %collective-permute-start.15) | collective-permute-done | bytes 131104 | tf_op jit(solution)/shard_map/ppermute | solution.py:321
  116.9 3.8 %all-to-all-done.1 = f32[16,128,256]{2,1,0:T(8,128)S(1)} async-done(((f32[16,128,256]{2,1,0:T(8,128)}), f32[16,128,256]{2,1,0:T(8,128)S(1)}, u32[]{:S(2)}, u32[]{:S(2)}) %all-to-all-start.1) | async-done | bytes 2097184 | tf_op jit(solution)/shard_map/all_to_all | solution.py:329
  121.3 5.8 %collective-permute-start.18 = (f32[128,128]{1,0:T(8,128)S(1)}, f32[128,128]{1,0:T(8,128)S(1)}, u32[]{:S(2)}, u32[]{:S(2)}) collective-permute-start(f32[128,128]{1,0:T(8,128)S(1)} %small.1), channel_id=1, source_target_pairs={{0,1},{1,0},{2,3},{3,2},{4,5},{5,4},{6,7},{7,6},{8,9},{9,8},{10,11... | collective-permute-start | bytes 196616 | tf_op jit(solution)/shard_map/ppermute | solution.py:369
  128.0 1.5 %collective-permute-start.21 = (f32[128,128]{1,0:T(8,128)S(1)}, f32[128,128]{1,0:T(8,128)S(1)}, u32[]{:S(2)}, u32[]{:S(2)}) collective-permute-start(f32[128,128]{1,0:T(8,128)S(1)} %add.37.refs_0_), channel_id=1, source_target_pairs={{0,6},{1,7},{2,0},{3,1},{4,2},{5,3},{6,4},{7,5},{8,14},{9,15},{10,... | collective-permute-start | bytes 196616 | tf_op jit(solution)/shard_map/ppermute | solution.py:321
  129.5 1.4 collective-permute-start.20
  131.6 2.5 %collective-permute-done.20.refs_2_ = f32[128,128]{1,0:T(8,128)S(1)} collective-permute-done((f32[128,128]{1,0:T(8,128)S(1)}, f32[128,128]{1,0:T(8,128)S(1)}, u32[]{:S(2)}, u32[]{:S(2)}) %collective-permute-start.20) | collective-permute-done | bytes 65568 | tf_op jit(solution)/shard_map/ppermute | solution.py:321
  134.1 1.8 %collective-permute-done.19.refs_1_ = f32[128,128]{1,0:T(8,128)S(1)} collective-permute-done((f32[128,128]{1,0:T(8,128)S(1)}, f32[128,128]{1,0:T(8,128)S(1)}, u32[]{:S(2)}, u32[]{:S(2)}) %collective-permute-start.19) | collective-permute-done | bytes 65568 | tf_op jit(solution)/shard_map/ppermute | solution.py:321
  136.0 0.9 copy-done.6
  136.9 10.1 %update.1 = f32[1024,2048]{1,0:T(8,128)} custom-call(f32[1024,2048]{1,0:T(8,128)} %a_ref.3, f32[8,2,128,256]{3,2,1,0:T(8,128)S(1)} %bitcast.6, f32[1024,128]{1,0:T(8,128)S(1)} %get-tuple-element.11.v_ref, bf16[1024,128]{1,0:T(8,128)(2,1)S(1)} %get-tuple-element.13.after_ref.th_ref, bf16[1024,128]{1,0:T(8,128)(2,1)S(1)} %copy-done.6, ...), custom_call_target="tpu_custom_call" | custom-call | flops 3221225472 | bytes 16777216 | tf_op jit(solution)/shard_map/update/pallas_call | solution.py:282
  (60 shorter events, 16.4 us)
Async XLA Ops:
  0.6 1.0 copy-start.1
  2.3 10.1 %collective-permute-start.2 = (f32[128,128]{1,0:T(8,128)S(1)}, f32[128,128]{1,0:T(8,128)S(1)}, u32[]{:S(2)}, u32[]{:S(2)}) collective-permute-start(f32[128,128]{1,0:T(8,128)S(1)} %gram.1), channel_id=1, source_target_pairs={{0,24},{8,0},{16,8},{24,16},{32,56},{40,32},{48,40},{56,48},{64,88... | collective-permute-start | bytes 196616 | tf_op jit(solution)/shard_map/ppermute | solution.py:321
  5.7 8.0 %collective-permute-start.1 = (f32[128,128]{1,0:T(8,128)S(1)}, f32[128,128]{1,0:T(8,128)S(1)}, u32[]{:S(2)}, u32[]{:S(2)}) collective-permute-start(f32[128,128]{1,0:T(8,128)S(1)} %gram.1), channel_id=1, source_target_pairs={{0,8},{8,16},{16,24},{24,0},{32,40},{40,48},{48,56},{56,32},{64,72... | collective-permute-start | bytes 196616 | tf_op jit(solution)/shard_map/ppermute | solution.py:321
  5.7 8.1 %collective-permute-start = (f32[128,128]{1,0:T(8,128)S(1)}, f32[128,128]{1,0:T(8,128)S(1)}, u32[]{:S(2)}, u32[]{:S(2)}) collective-permute-start(f32[128,128]{1,0:T(8,128)S(1)} %gram.1), channel_id=1, source_target_pairs={{0,16},{8,24},{16,0},{24,8},{32,48},{40,56},{48,32},{56,40},{64,80... | collective-permute-start | bytes 196616 | tf_op jit(solution)/shard_map/ppermute | solution.py:321
  8.3 6.4 %collective-permute-start.8 = (f32[128,128]{1,0:T(8,128)S(1)}, f32[128,128]{1,0:T(8,128)S(1)}, u32[]{:S(2)}, u32[]{:S(2)}) collective-permute-start(f32[128,128]{1,0:T(8,128)S(1)} %slice_select_fusion), channel_id=1, source_target_pairs={{0,24},{1,25},{2,26},{3,27},{4,28},{5,29},{6,30},{7,31}} | collective-permute-start | bytes 196616 | tf_op jit(solution)/shard_map/ppermute | solution.py:348
  11.1 4.3 %collective-permute-start.7 = (f32[128,128]{1,0:T(8,128)S(1)}, f32[128,128]{1,0:T(8,128)S(1)}, u32[]{:S(2)}, u32[]{:S(2)}) collective-permute-start(f32[128,128]{1,0:T(8,128)S(1)} %slice_select_fusion), channel_id=1, source_target_pairs={{0,16},{1,17},{2,18},{3,19},{4,20},{5,21},{6,22},{7,23}} | collective-permute-start | bytes 196616 | tf_op jit(solution)/shard_map/ppermute | solution.py:348
  12.4 3.0 %collective-permute-start.6 = (f32[128,128]{1,0:T(8,128)S(1)}, f32[128,128]{1,0:T(8,128)S(1)}, u32[]{:S(2)}, u32[]{:S(2)}) collective-permute-start(f32[128,128]{1,0:T(8,128)S(1)} %slice_select_fusion), channel_id=1, source_target_pairs={{0,8},{1,9},{2,10},{3,11},{4,12},{5,13},{6,14},{7,15}} | collective-permute-start | bytes 196616 | tf_op jit(solution)/shard_map/ppermute | solution.py:348
  13.8 8.6 %collective-permute-start.5 = (f32[128,128]{1,0:T(8,128)S(1)}, f32[128,128]{1,0:T(8,128)S(1)}, u32[]{:S(2)}, u32[]{:S(2)}) collective-permute-start(f32[128,128]{1,0:T(8,128)S(1)} %add_add_fusion.1.a_ref), channel_id=1, source_target_pairs={{0,96},{8,104},{16,112},{24,120},{32,0},{40,8},{48,16},{56,24},{64... | collective-permute-start | bytes 196616 | tf_op jit(solution)/shard_map/ppermute | solution.py:321
  14.7 9.0 %collective-permute-start.4 = (f32[128,128]{1,0:T(8,128)S(1)}, f32[128,128]{1,0:T(8,128)S(1)}, u32[]{:S(2)}, u32[]{:S(2)}) collective-permute-start(f32[128,128]{1,0:T(8,128)S(1)} %add_add_fusion.1.a_ref), channel_id=1, source_target_pairs={{0,64},{8,72},{16,80},{24,88},{32,96},{40,104},{48,112},{56,120},{... | collective-permute-start | bytes 196616 | tf_op jit(solution)/shard_map/ppermute | solution.py:321
  14.7 9.0 %collective-permute-start.3 = (f32[128,128]{1,0:T(8,128)S(1)}, f32[128,128]{1,0:T(8,128)S(1)}, u32[]{:S(2)}, u32[]{:S(2)}) collective-permute-start(f32[128,128]{1,0:T(8,128)S(1)} %add_add_fusion.1.a_ref), channel_id=1, source_target_pairs={{0,32},{8,40},{16,48},{24,56},{32,64},{40,72},{48,80},{56,88},{64,... | collective-permute-start | bytes 196616 | tf_op jit(solution)/shard_map/ppermute | solution.py:321
  16.3 35.3 %collective-permute-start.11 = (f32[128,128]{1,0:T(8,128)S(1)}, f32[128,128]{1,0:T(8,128)S(1)}, u32[]{:S(2)}, u32[]{:S(2)}) collective-permute-start(f32[128,128]{1,0:T(8,128)S(1)} %add_add_fusion.refs_0_), channel_id=1, source_target_pairs={{0,96},{8,104},{16,112},{24,120},{1,97},{9,105},{17,113},{25,121},... | collective-permute-start | bytes 196616 | tf_op jit(solution)/shard_map/ppermute | solution.py:350
  20.5 31.1 %collective-permute-start.10 = (f32[128,128]{1,0:T(8,128)S(1)}, f32[128,128]{1,0:T(8,128)S(1)}, u32[]{:S(2)}, u32[]{:S(2)}) collective-permute-start(f32[128,128]{1,0:T(8,128)S(1)} %add_add_fusion.refs_0_), channel_id=1, source_target_pairs={{0,64},{8,72},{16,80},{24,88},{1,65},{9,73},{17,81},{25,89},{2,66}... | collective-permute-start | bytes 196616 | tf_op jit(solution)/shard_map/ppermute | solution.py:350
  22.4 29.2 %collective-permute-start.9 = (f32[128,128]{1,0:T(8,128)S(1)}, f32[128,128]{1,0:T(8,128)S(1)}, u32[]{:S(2)}, u32[]{:S(2)}) collective-permute-start(f32[128,128]{1,0:T(8,128)S(1)} %add_add_fusion.refs_0_), channel_id=1, source_target_pairs={{0,32},{8,40},{16,48},{24,56},{1,33},{9,41},{17,49},{25,57},{2,34}... | collective-permute-start | bytes 196616 | tf_op jit(solution)/shard_map/ppermute | solution.py:350
  51.6 1.0 copy-start.2
  58.3 18.2 %all-to-all-start = ((f32[16,128,128]{2,1,0:T(8,128)}), f32[16,128,128]{2,1,0:T(8,128)S(1)}, u32[]{:S(2)}, u32[]{:S(2)}) async-start(f32[16,128,128]{2,1,0:T(8,128)} %bitcast.1), calls=%async_computation | async-start | bytes 2097152 | tf_op jit(solution)/shard_map/all_to_all | solution.py:329
  61.9 20.5 %collective-permute-start.12 = (f32[128,128]{1,0:T(8,128)S(1)}, f32[128,128]{1,0:T(8,128)S(1)}, u32[]{:S(2)}, u32[]{:S(2)}) collective-permute-start(f32[128,128]{1,0:T(8,128)S(1)} %constant_dynamic-slice_fusion), channel_id=1, source_target_pairs={{0,0},{16,1},{32,2},{48,3},{64,4},{80,5},{96,6},{112,7},{8,8},{24,... | collective-permute-start | bytes 196616 | tf_op jit(solution)/shard_map/ppermute | solution.py:355
  74.8 11.1 %copy-start.5 = (bf16[1024,128]{1,0:T(8,128)(2,1)}, bf16[1024,128]{1,0:T(8,128)(2,1)S(1)}, u32[]{:S(2)}) copy-start(bf16[1024,128]{1,0:T(8,128)(2,1)S(1)} %get-tuple-element.14.tl_ref) | copy-start | bytes 786436
  76.6 7.7 %collective-permute-start.13 = (f32[128,128]{1,0:T(8,128)S(1)}, f32[128,128]{1,0:T(8,128)S(1)}, u32[]{:S(2)}, u32[]{:S(2)}) collective-permute-start(f32[128,128]{1,0:T(8,128)S(1)} %chunk.1.w_ref), channel_id=1, source_target_pairs={{0,0},{16,1},{32,2},{48,3},{64,4},{80,5},{96,6},{112,7},{8,8},{24,... | collective-permute-start | bytes 196616 | tf_op jit(solution)/shard_map/ppermute | solution.py:361
  84.5 1.3 copy-start
  85.8 34.8 %all-to-all-start.1 = ((f32[16,128,256]{2,1,0:T(8,128)}), f32[16,128,256]{2,1,0:T(8,128)S(1)}, u32[]{:S(2)}, u32[]{:S(2)}) async-start(f32[16,128,256]{2,1,0:T(8,128)} %copy-done), calls=%async_computation.1 | async-start | bytes 4194304 | tf_op jit(solution)/shard_map/all_to_all | solution.py:329
  95.4 3.9 %collective-permute-start.14 = (f32[128,128]{1,0:T(8,128)S(1)}, f32[128,128]{1,0:T(8,128)S(1)}, u32[]{:S(2)}, u32[]{:S(2)}) collective-permute-start(f32[128,128]{1,0:T(8,128)S(1)} %collective-permute-done.13.after_ref), channel_id=1, source_target_pairs={{0,1},{1,0},{2,3},{3,2},{4,5},{5,4},{6,7},{7,6},{8,9},{9,8},{10,11... | collective-permute-start | bytes 196616 | tf_op jit(solution)/shard_map/ppermute | solution.py:364
  99.3 7.9 %collective-permute-start.17 = (f32[256,128]{1,0:T(8,128)S(1)}, f32[256,128]{1,0:T(8,128)S(1)}, u32[]{:S(2)}, u32[]{:S(2)}) collective-permute-start(f32[256,128]{1,0:T(8,128)S(1)} %pad_maximum_fusion.refs_0_), channel_id=1, source_target_pairs={{0,6},{1,7},{2,0},{3,1},{4,2},{5,3},{6,4},{7,5},{8,14},{9,15},{10,... | collective-permute-start | bytes 393224 | tf_op jit(solution)/shard_map/ppermute | solution.py:321
  102.0 5.9 %collective-permute-start.16 = (f32[256,128]{1,0:T(8,128)S(1)}, f32[256,128]{1,0:T(8,128)S(1)}, u32[]{:S(2)}, u32[]{:S(2)}) collective-permute-start(f32[256,128]{1,0:T(8,128)S(1)} %pad_maximum_fusion.refs_0_), channel_id=1, source_target_pairs={{0,4},{1,5},{2,6},{3,7},{4,0},{5,1},{6,2},{7,3},{8,12},{9,13},{10,... | collective-permute-start | bytes 393224 | tf_op jit(solution)/shard_map/ppermute | solution.py:321
  102.7 9.0 %collective-permute-start.15 = (f32[256,128]{1,0:T(8,128)S(1)}, f32[256,128]{1,0:T(8,128)S(1)}, u32[]{:S(2)}, u32[]{:S(2)}) collective-permute-start(f32[256,128]{1,0:T(8,128)S(1)} %pad_maximum_fusion.refs_0_), channel_id=1, source_target_pairs={{0,2},{1,3},{2,4},{3,5},{4,6},{5,7},{6,0},{7,1},{8,10},{9,11},{10,... | collective-permute-start | bytes 393224 | tf_op jit(solution)/shard_map/ppermute | solution.py:321
  112.4 0.9 copy-start.4
  113.3 0.9 copy-start.8
  114.2 0.9 copy-start.10
  121.3 6.7 %collective-permute-start.18 = (f32[128,128]{1,0:T(8,128)S(1)}, f32[128,128]{1,0:T(8,128)S(1)}, u32[]{:S(2)}, u32[]{:S(2)}) collective-permute-start(f32[128,128]{1,0:T(8,128)S(1)} %small.1), channel_id=1, source_target_pairs={{0,1},{1,0},{2,3},{3,2},{4,5},{5,4},{6,7},{7,6},{8,9},{9,8},{10,11... | collective-permute-start | bytes 196616 | tf_op jit(solution)/shard_map/ppermute | solution.py:369
  128.0 3.6 %collective-permute-start.21 = (f32[128,128]{1,0:T(8,128)S(1)}, f32[128,128]{1,0:T(8,128)S(1)}, u32[]{:S(2)}, u32[]{:S(2)}) collective-permute-start(f32[128,128]{1,0:T(8,128)S(1)} %add.37.refs_0_), channel_id=1, source_target_pairs={{0,6},{1,7},{2,0},{3,1},{4,2},{5,3},{6,4},{7,5},{8,14},{9,15},{10,... | collective-permute-start | bytes 196616 | tf_op jit(solution)/shard_map/ppermute | solution.py:321
  129.5 4.6 %collective-permute-start.20 = (f32[128,128]{1,0:T(8,128)S(1)}, f32[128,128]{1,0:T(8,128)S(1)}, u32[]{:S(2)}, u32[]{:S(2)}) collective-permute-start(f32[128,128]{1,0:T(8,128)S(1)} %add.37.refs_0_), channel_id=1, source_target_pairs={{0,4},{1,5},{2,6},{3,7},{4,0},{5,1},{6,2},{7,3},{8,12},{9,13},{10,... | collective-permute-start | bytes 196616 | tf_op jit(solution)/shard_map/ppermute | solution.py:321
  131.0 5.0 %collective-permute-start.19 = (f32[128,128]{1,0:T(8,128)S(1)}, f32[128,128]{1,0:T(8,128)S(1)}, u32[]{:S(2)}, u32[]{:S(2)}) collective-permute-start(f32[128,128]{1,0:T(8,128)S(1)} %add.37.refs_0_), channel_id=1, source_target_pairs={{0,2},{1,3},{2,4},{3,5},{4,6},{5,7},{6,0},{7,1},{8,10},{9,11},{10,... | collective-permute-start | bytes 196616 | tf_op jit(solution)/shard_map/ppermute | solution.py:321
  136.0 1.0 copy-start.6
  (5 other events, 3.5 us)

commit v3 on v2

--- a/solution.py
+++ b/solution.py
@@ -57,10 +57,11 @@
     x = one
     err = corr - one
     for step in range(STEPS):
+        dot = hdot if step >= STEPS - 2 else dot3
         if step:
-            err = hdot(hdot(x, corr), x, ((1,), (1,))) - one
+            err = dot(dot(x, corr), x, ((1,), (1,))) - one
         phi = jnp.where(r > c, err, jnp.where(r == c, 0.5 * err, 0.0))
-        x = x - (phi if step == 0 else hdot(phi, x))
+        x = x - (phi if step == 0 else dot(phi, x))
     out_ref[...] = x * scale_row
     size = jnp.sum(err * err)
     good = size < 1e-8
@@ -255,46 +256,45 @@
 
 def update_kernel(trailing, right, v, turned, mixed, coupling, parts):
     rows, cols = trailing.shape
-    tile = 512
-    chunks = tile // B
+    tile = rows // 2
+    halves = right.shape[1]
+    wide = cols // halves
 
     def body(a_ref, right_ref, v_ref, th_ref, tl_ref, m_ref, t_ref, *refs):
-        s_refs, (out_ref, h_ref, l_ref) = refs[:YN], refs[YN:]
+        s_refs, (out_ref, small_ref, rh_ref, rl_ref) = refs[:YN], refs[YN:]
 
         @pl.when(pl.program_id(0) == 0)
         def _():
             t = t_ref[...]
             s = [ref[...] for ref in s_refs]
             small = hdot(hdot(t, (s[0] + s[2]) + (s[1] + s[3]), ((0,), (0,))), t)
-            small = 0.5 * (small + small.T)
-            h_ref[:, :B], l_ref[:, :B] = th_ref[...], tl_ref[...]
-            h_ref[:, B:], l_ref[:, B:] = split(m_ref[...] - dot3(v_ref[...], small))
-
-        rh, rl = split(right_ref[...].reshape(tile, 2 * B))
-        h = h_ref[...]
+            small_ref[...] = 0.5 * (small + small.T)
+            for h in range(halves):
+                at = slice(h * wide, (h + 1) * wide)
+                rh_ref[at], rl_ref[at] = split(right_ref[:, h].reshape(wide, 2 * B))
+
+        high, low = split(m_ref[...] - dot3(v_ref[...], small_ref[...]))
+        high = jnp.concatenate([th_ref[...], high], axis=1)
+        low = jnp.concatenate([tl_ref[...], low], axis=1)
         nt = ((1,), (1,))
-        out_ref[...] = a_ref[...] - (bdot(h, rh, nt) + (bdot(h, rl, nt) + bdot(l_ref[...], rh, nt)))
+        for k in range(0, cols, 512):
+            at = slice(k, k + 512)
+            rh, rl = rh_ref[at], rl_ref[at]
+            out_ref[:, at] = a_ref[:, at] - (bdot(high, rh, nt) + (bdot(high, rl, nt) + bdot(low, rh, nt)))
 
     def whole(*shape):
-        return pl.BlockSpec(shape, lambda t: (0, 0))
-
-    per_half = right.shape[0] // chunks
-    return pl.pallas_call(
-        body,
-        grid=(cols // tile,),
+        return pl.BlockSpec(shape, lambda t: (0,) * len(shape))
+
+    def mine(width):
+        return pl.BlockSpec((tile, width), lambda t: (t, 0))
+
+    return pl.pallas_call(
+        body,
+        grid=(rows // tile,),
         out_shape=shaped(rows, cols),
-        in_specs=[
-            pl.BlockSpec((rows, tile), lambda t: (0, t)),
-            pl.BlockSpec((chunks, 1, B, 2 * B), lambda t: (t % per_half, t // per_half, 0, 0)),
-            whole(rows, B),
-            whole(rows, B),
-            whole(rows, B),
-            whole(rows, B),
-            whole(B, B),
-        ]
-        + [whole(B, B)] * YN,
-        out_specs=pl.BlockSpec((rows, tile), lambda t: (0, t)),
-        scratch_shapes=[pltpu.VMEM((rows, 2 * B), BF16)] * 2,
+        in_specs=[mine(cols), whole(*right.shape), mine(B), mine(B), mine(B), mine(B), whole(B, B)] + [whole(B, B)] * YN,
+        out_specs=mine(cols),
+        scratch_shapes=[pltpu.VMEM((B, B), F32)] + [pltpu.VMEM((cols, 2 * B), BF16)] * 2,
         compiler_params=params(),
         cost_estimate=pl.CostEstimate(flops=12 * rows * cols * B, bytes_accessed=8 * rows * cols, transcendentals=0),
         name="update",

time: 148 us -> 146 us (0.986)
  Pallas kernels: 51.2 us -> 49.5 us
  transfers between devices with their start and end apart: 24 -> 24, of which waited for: 10 -> 11; matrix products, arithmetic and copies ran while one was open for 1% -> 1% of each run, Pallas kernels for 23% -> 23%
where the time goes in v3:
time: 146 us
  starting transfers between devices  62 us (42%)
  Pallas kernels  49.5 us (34%)
  waiting for transfers between devices  20.8 us (14%)
  local copies, waits for them, and re-layouts  10.6 us (7%)
  other arithmetic  1.83 us (1%)
    pallas_call x1, Pallas kernels, factor_kernel(): pl.pallas_call(body, out_shape=(square, square), scratch_shapes=[pltpu.VM...  27.3 us
    ppermute x12, starting transfers between devices, four(): return [value] + [lax.ppermute(value, axis, along(d)) for d in (1, 2, 3)]  13.9 us
    all_to_all x2, starting transfers between devices, to_all(): return lax.all_to_all(copies, axis, split_axis=0, concat_axis=0, tiled=True)  13.2 us
    ppermute x12, waiting for transfers between devices, four(): return [value] + [lax.ppermute(value, axis, along(d)) for d in (1, 2, 3)]  11 us
    unnamed x26, local copies, waits for them, and re-layouts  10.6 us
    pallas_call x1, Pallas kernels, update_kernel(): pl.pallas_call(body, grid=(rows // tile,), out_shape=shaped(rows, cols),...  9.55 us
    ppermute x1, starting transfers between devices, shards(): lax.ppermute(lax.dynamic_slice_in_dim(v, j * B, B, 0), ('prow', 'pcol'),...  7.64 us
    ppermute x3, starting transfers between devices, shards(): lax.ppermute(top, 'prow', [(k, z * XN + k) for k in range(XN)])  7.37 us
  transfers between devices with their start and end apart: 24, of which 11 were waited for; matrix products, arithmetic and copies ran while one was open for 1% of the time, Pallas kernels for 23%

profile of v3, /device:TPU:1, one launch (start us, length us, event | category | flops | bytes accessed | tf_op | source)
XLA Modules:
  0.0 145.7 jit_solution(14312086996449268997)
XLA Ops:
  0.6 1.0 copy-done.1
  2.3 3.4 %collective-permute-start.2 = (f32[128,128]{1,0:T(8,128)S(1)}, f32[128,128]{1,0:T(8,128)S(1)}, u32[]{:S(2)}, u32[]{:S(2)}) collective-permute-start(f32[128,128]{1,0:T(8,128)S(1)} %gram.1), channel_id=1, source_target_pairs={{0,24},{8,0},{16,8},{24,16},{32,56},{40,32},{48,40},{56,48},{64,88... | collective-permute-start | bytes 196616 | tf_op jit(solution)/shard_map/ppermute | solution.py:321
  5.7 1.7 %collective-permute-start = (f32[128,128]{1,0:T(8,128)S(1)}, f32[128,128]{1,0:T(8,128)S(1)}, u32[]{:S(2)}, u32[]{:S(2)}) collective-permute-start(f32[128,128]{1,0:T(8,128)S(1)} %gram.1), channel_id=1, source_target_pairs={{0,16},{8,24},{16,0},{24,8},{32,48},{40,56},{48,32},{56,40},{64,80... | collective-permute-start | bytes 196616 | tf_op jit(solution)/shard_map/ppermute | solution.py:321
  8.3 2.8 %collective-permute-start.8 = (f32[128,128]{1,0:T(8,128)S(1)}, f32[128,128]{1,0:T(8,128)S(1)}, u32[]{:S(2)}, u32[]{:S(2)}) collective-permute-start(f32[128,128]{1,0:T(8,128)S(1)} %slice_select_fusion), channel_id=1, source_target_pairs={{0,24},{1,25},{2,26},{3,27},{4,28},{5,29},{6,30},{7,31}} | collective-permute-start | bytes 196616 | tf_op jit(solution)/shard_map/ppermute | solution.py:348
  11.1 1.3 collective-permute-start.7
  12.4 1.3 collective-permute-start.6
  16.3 4.2 %collective-permute-start.11 = (f32[128,128]{1,0:T(8,128)S(1)}, f32[128,128]{1,0:T(8,128)S(1)}, u32[]{:S(2)}, u32[]{:S(2)}) collective-permute-start(f32[128,128]{1,0:T(8,128)S(1)} %add_add_fusion.refs_0_), channel_id=1, source_target_pairs={{0,96},{8,104},{16,112},{24,120},{1,97},{9,105},{17,113},{25,121},... | collective-permute-start | bytes 196616 | tf_op jit(solution)/shard_map/ppermute | solution.py:350
  20.5 1.8 %collective-permute-start.10 = (f32[128,128]{1,0:T(8,128)S(1)}, f32[128,128]{1,0:T(8,128)S(1)}, u32[]{:S(2)}, u32[]{:S(2)}) collective-permute-start(f32[128,128]{1,0:T(8,128)S(1)} %add_add_fusion.refs_0_), channel_id=1, source_target_pairs={{0,64},{8,72},{16,80},{24,88},{1,65},{9,73},{17,81},{25,89},{2,66}... | collective-permute-start | bytes 196616 | tf_op jit(solution)/shard_map/ppermute | solution.py:350
  22.4 1.3 collective-permute-start.9
  23.7 27.3 %factor.1 = (f32[128,128]{1,0:T(8,128)}, f32[128,128]{1,0:T(8,128)S(1)}) custom-call(f32[128,128]{1,0:T(8,128)S(1)} %add_add_fusion.1.a_ref, f32[128,128]{1,0:T(8,128)S(1)} %collective-permute-done.3.b_ref, f32[128,128]{1,0:T(8,128)S(1)} %collective-permute-done.4.c_ref, f32[128,128]{1,0:T(8,128)S(1)} %collective-permute-done.5.d_ref), custom_call_target="tpu_custom_call" | custom-call | tf_op jit(solution)/shard_map/factor/pallas_call | solution.py:167
  51.0 1.0 copy-done.2
  52.0 5.6 %product.1 = (f32[1024,128]{1,0:T(8,128)S(1)}, f32[8,2,128,128]{3,2,1,0:T(8,128)}) custom-call(s32[1]{0:T(128)} %bitcast.first_ref, f32[1024,128]{1,0:T(8,128)S(1)} %copy-done.2, f32[128,128]{1,0:T(8,128)S(1)} %get-tuple-element.9.r_ref.refs_4_, f32[1024,2048]{1,0:T(8,128)} %a_ref.3, f32[128,128]{1,0:T(8,128)S(1)} %add_add_fusion.refs_0_, ...), custom_call_target="tpu_custom_call" | custom-call | flops 1610612736 | bytes 8388608 | tf_op jit(solution)/shard_map/product/pallas_call | solution.py:135
  57.7 3.7 %all-to-all-start = ((f32[16,128,128]{2,1,0:T(8,128)}), f32[16,128,128]{2,1,0:T(8,128)S(1)}, u32[]{:S(2)}, u32[]{:S(2)}) async-start(f32[16,128,128]{2,1,0:T(8,128)} %bitcast.1), calls=%async_computation | async-start | bytes 2097152 | tf_op jit(solution)/shard_map/all_to_all | solution.py:329
  61.4 7.6 %collective-permute-start.12 = (f32[128,128]{1,0:T(8,128)S(1)}, f32[128,128]{1,0:T(8,128)S(1)}, u32[]{:S(2)}, u32[]{:S(2)}) collective-permute-start(f32[128,128]{1,0:T(8,128)S(1)} %constant_dynamic-slice_fusion), channel_id=1, source_target_pairs={{0,0},{16,1},{32,2},{48,3},{64,4},{80,5},{96,6},{112,7},{8,8},{24,... | collective-permute-start | bytes 196616 | tf_op jit(solution)/shard_map/ppermute | solution.py:355
  69.0 4.2 %coupling.1.t_ref = f32[128,128]{1,0:T(8,128)S(1)} custom-call(f32[128,128]{1,0:T(8,128)S(1)} %add_add_fusion.refs_0_, f32[128,128]{1,0:T(8,128)S(1)} %collective-permute-done.9.refs_1_, f32[128,128]{1,0:T(8,128)S(1)} %collective-permute-done.10.refs_2_, f32[128,128]{1,0:T(8,128)S(1)} %collective-permute-done.11.refs_3_, ...), custom_call_target="tpu_custom_call" | custom-call | tf_op jit(solution)/shard_map/coupling/pallas_call | solution.py:240
  73.6 2.3 %all-to-all-done.y_ref = f32[16,128,128]{2,1,0:T(8,128)S(1)} async-done(((f32[16,128,128]{2,1,0:T(8,128)}), f32[16,128,128]{2,1,0:T(8,128)S(1)}, u32[]{:S(2)}, u32[]{:S(2)}) %all-to-all-start) | async-done | bytes 1048608 | tf_op jit(solution)/shard_map/all_to_all | solution.py:329
  76.0 5.8 %collective-permute-start.13 = (f32[128,128]{1,0:T(8,128)S(1)}, f32[128,128]{1,0:T(8,128)S(1)}, u32[]{:S(2)}, u32[]{:S(2)}) collective-permute-start(f32[128,128]{1,0:T(8,128)S(1)} %chunk.1.w_ref), channel_id=1, source_target_pairs={{0,0},{16,1},{32,2},{48,3},{64,4},{80,5},{96,6},{112,7},{8,8},{24,... | collective-permute-start | bytes 196616 | tf_op jit(solution)/shard_map/ppermute | solution.py:361
  81.8 1.9 %collective-permute-done.13.after_ref = f32[128,128]{1,0:T(8,128)S(1)} collective-permute-done((f32[128,128]{1,0:T(8,128)S(1)}, f32[128,128]{1,0:T(8,128)S(1)}, u32[]{:S(2)}, u32[]{:S(2)}) %collective-permute-start.13) | collective-permute-done | bytes 65568 | tf_op jit(solution)/shard_map/ppermute | solution.py:361
  83.9 1.3 copy-done
  85.3 9.5 %all-to-all-start.1 = ((f32[16,128,256]{2,1,0:T(8,128)}), f32[16,128,256]{2,1,0:T(8,128)S(1)}, u32[]{:S(2)}, u32[]{:S(2)}) async-start(f32[16,128,256]{2,1,0:T(8,128)} %copy-done), calls=%async_computation.1 | async-start | bytes 4194304 | tf_op jit(solution)/shard_map/all_to_all | solution.py:329
  94.8 3.0 %collective-permute-start.14 = (f32[128,128]{1,0:T(8,128)S(1)}, f32[128,128]{1,0:T(8,128)S(1)}, u32[]{:S(2)}, u32[]{:S(2)}) collective-permute-start(f32[128,128]{1,0:T(8,128)S(1)} %collective-permute-done.13.after_ref), channel_id=1, source_target_pairs={{0,1},{1,0},{2,3},{3,2},{4,5},{5,4},{6,7},{7,6},{8,9},{9,8},{10,11... | collective-permute-start | bytes 196616 | tf_op jit(solution)/shard_map/ppermute | solution.py:364
  98.7 2.7 %collective-permute-start.17 = (f32[256,128]{1,0:T(8,128)S(1)}, f32[256,128]{1,0:T(8,128)S(1)}, u32[]{:S(2)}, u32[]{:S(2)}) collective-permute-start(f32[256,128]{1,0:T(8,128)S(1)} %pad_maximum_fusion.refs_0_), channel_id=1, source_target_pairs={{0,6},{1,7},{2,0},{3,1},{4,2},{5,3},{6,4},{7,5},{8,14},{9,15},{10,... | collective-permute-start | bytes 393224 | tf_op jit(solution)/shard_map/ppermute | solution.py:321
  103.5 3.1 %collective-permute-done.17.refs_3_ = f32[256,128]{1,0:T(8,128)S(1)} collective-permute-done((f32[256,128]{1,0:T(8,128)S(1)}, f32[256,128]{1,0:T(8,128)S(1)}, u32[]{:S(2)}, u32[]{:S(2)}) %collective-permute-start.17) | collective-permute-done | bytes 131104 | tf_op jit(solution)/shard_map/ppermute | solution.py:321
  108.0 3.2 %collective-permute-done.15.refs_1_ = f32[256,128]{1,0:T(8,128)S(1)} collective-permute-done((f32[256,128]{1,0:T(8,128)S(1)}, f32[256,128]{1,0:T(8,128)S(1)}, u32[]{:S(2)}, u32[]{:S(2)}) %collective-permute-start.15) | collective-permute-done | bytes 131104 | tf_op jit(solution)/shard_map/ppermute | solution.py:321
  116.3 3.8 %all-to-all-done.1 = f32[16,128,256]{2,1,0:T(8,128)S(1)} async-done(((f32[16,128,256]{2,1,0:T(8,128)}), f32[16,128,256]{2,1,0:T(8,128)S(1)}, u32[]{:S(2)}, u32[]{:S(2)}) %all-to-all-start.1) | async-done | bytes 2097184 | tf_op jit(solution)/shard_map/all_to_all | solution.py:329
  120.7 5.8 %collective-permute-start.18 = (f32[128,128]{1,0:T(8,128)S(1)}, f32[128,128]{1,0:T(8,128)S(1)}, u32[]{:S(2)}, u32[]{:S(2)}) collective-permute-start(f32[128,128]{1,0:T(8,128)S(1)} %small.1), channel_id=1, source_target_pairs={{0,1},{1,0},{2,3},{3,2},{4,5},{5,4},{6,7},{7,6},{8,9},{9,8},{10,11... | collective-permute-start | bytes 196616 | tf_op jit(solution)/shard_map/ppermute | solution.py:369
  127.4 1.2 collective-permute-start.21
  128.6 1.5 %collective-permute-start.20 = (f32[128,128]{1,0:T(8,128)S(1)}, f32[128,128]{1,0:T(8,128)S(1)}, u32[]{:S(2)}, u32[]{:S(2)}) collective-permute-start(f32[128,128]{1,0:T(8,128)S(1)} %add.37.refs_0_), channel_id=1, source_target_pairs={{0,4},{1,5},{2,6},{3,7},{4,0},{5,1},{6,2},{7,3},{8,12},{9,13},{10,... | collective-permute-start | bytes 196616 | tf_op jit(solution)/shard_map/ppermute | solution.py:321
  130.6 2.6 %collective-permute-done.20.refs_2_ = f32[128,128]{1,0:T(8,128)S(1)} collective-permute-done((f32[128,128]{1,0:T(8,128)S(1)}, f32[128,128]{1,0:T(8,128)S(1)}, u32[]{:S(2)}, u32[]{:S(2)}) %collective-permute-start.20) | collective-permute-done | bytes 65568 | tf_op jit(solution)/shard_map/ppermute | solution.py:321
  133.2 2.0 %collective-permute-done.19.refs_1_ = f32[128,128]{1,0:T(8,128)S(1)} collective-permute-done((f32[128,128]{1,0:T(8,128)S(1)}, f32[128,128]{1,0:T(8,128)S(1)}, u32[]{:S(2)}, u32[]{:S(2)}) %collective-permute-start.19) | collective-permute-done | bytes 65568 | tf_op jit(solution)/shard_map/ppermute | solution.py:321
  135.2 0.9 copy-done.6
  136.1 9.5 %update.1 = f32[1024,2048]{1,0:T(8,128)} custom-call(f32[1024,2048]{1,0:T(8,128)} %a_ref.3, f32[8,2,128,256]{3,2,1,0:T(8,128)S(1)} %bitcast.6, f32[1024,128]{1,0:T(8,128)S(1)} %get-tuple-element.11.v_ref, bf16[1024,128]{1,0:T(8,128)(2,1)S(1)} %get-tuple-element.13.after_ref.th_ref, bf16[1024,128]{1,0:T(8,128)(2,1)S(1)} %copy-done.6, ...), custom_call_target="tpu_custom_call" | custom-call | flops 3221225472 | bytes 16777216 | tf_op jit(solution)/shard_map/update/pallas_call | solution.py:291
  (60 shorter events, 16.3 us)
Async XLA Ops:
  0.6 1.0 copy-start.1
  2.3 10.1 %collective-permute-start.2 = (f32[128,128]{1,0:T(8,128)S(1)}, f32[128,128]{1,0:T(8,128)S(1)}, u32[]{:S(2)}, u32[]{:S(2)}) collective-permute-start(f32[128,128]{1,0:T(8,128)S(1)} %gram.1), channel_id=1, source_target_pairs={{0,24},{8,0},{16,8},{24,16},{32,56},{40,32},{48,40},{56,48},{64,88... | collective-permute-start | bytes 196616 | tf_op jit(solution)/shard_map/ppermute | solution.py:321
  5.7 8.0 %collective-permute-start.1 = (f32[128,128]{1,0:T(8,128)S(1)}, f32[128,128]{1,0:T(8,128)S(1)}, u32[]{:S(2)}, u32[]{:S(2)}) collective-permute-start(f32[128,128]{1,0:T(8,128)S(1)} %gram.1), channel_id=1, source_target_pairs={{0,8},{8,16},{16,24},{24,0},{32,40},{40,48},{48,56},{56,32},{64,72... | collective-permute-start | bytes 196616 | tf_op jit(solution)/shard_map/ppermute | solution.py:321
  5.7 8.1 %collective-permute-start = (f32[128,128]{1,0:T(8,128)S(1)}, f32[128,128]{1,0:T(8,128)S(1)}, u32[]{:S(2)}, u32[]{:S(2)}) collective-permute-start(f32[128,128]{1,0:T(8,128)S(1)} %gram.1), channel_id=1, source_target_pairs={{0,16},{8,24},{16,0},{24,8},{32,48},{40,56},{48,32},{56,40},{64,80... | collective-permute-start | bytes 196616 | tf_op jit(solution)/shard_map/ppermute | solution.py:321
  8.3 6.4 %collective-permute-start.8 = (f32[128,128]{1,0:T(8,128)S(1)}, f32[128,128]{1,0:T(8,128)S(1)}, u32[]{:S(2)}, u32[]{:S(2)}) collective-permute-start(f32[128,128]{1,0:T(8,128)S(1)} %slice_select_fusion), channel_id=1, source_target_pairs={{0,24},{1,25},{2,26},{3,27},{4,28},{5,29},{6,30},{7,31}} | collective-permute-start | bytes 196616 | tf_op jit(solution)/shard_map/ppermute | solution.py:348
  11.1 4.3 %collective-permute-start.7 = (f32[128,128]{1,0:T(8,128)S(1)}, f32[128,128]{1,0:T(8,128)S(1)}, u32[]{:S(2)}, u32[]{:S(2)}) collective-permute-start(f32[128,128]{1,0:T(8,128)S(1)} %slice_select_fusion), channel_id=1, source_target_pairs={{0,16},{1,17},{2,18},{3,19},{4,20},{5,21},{6,22},{7,23}} | collective-permute-start | bytes 196616 | tf_op jit(solution)/shard_map/ppermute | solution.py:348
  12.4 3.0 %collective-permute-start.6 = (f32[128,128]{1,0:T(8,128)S(1)}, f32[128,128]{1,0:T(8,128)S(1)}, u32[]{:S(2)}, u32[]{:S(2)}) collective-permute-start(f32[128,128]{1,0:T(8,128)S(1)} %slice_select_fusion), channel_id=1, source_target_pairs={{0,8},{1,9},{2,10},{3,11},{4,12},{5,13},{6,14},{7,15}} | collective-permute-start | bytes 196616 | tf_op jit(solution)/shard_map/ppermute | solution.py:348
  13.8 8.6 %collective-permute-start.5 = (f32[128,128]{1,0:T(8,128)S(1)}, f32[128,128]{1,0:T(8,128)S(1)}, u32[]{:S(2)}, u32[]{:S(2)}) collective-permute-start(f32[128,128]{1,0:T(8,128)S(1)} %add_add_fusion.1.a_ref), channel_id=1, source_target_pairs={{0,96},{8,104},{16,112},{24,120},{32,0},{40,8},{48,16},{56,24},{64... | collective-permute-start | bytes 196616 | tf_op jit(solution)/shard_map/ppermute | solution.py:321
  14.7 9.0 %collective-permute-start.4 = (f32[128,128]{1,0:T(8,128)S(1)}, f32[128,128]{1,0:T(8,128)S(1)}, u32[]{:S(2)}, u32[]{:S(2)}) collective-permute-start(f32[128,128]{1,0:T(8,128)S(1)} %add_add_fusion.1.a_ref), channel_id=1, source_target_pairs={{0,64},{8,72},{16,80},{24,88},{32,96},{40,104},{48,112},{56,120},{... | collective-permute-start | bytes 196616 | tf_op jit(solution)/shard_map/ppermute | solution.py:321
  14.7 9.0 %collective-permute-start.3 = (f32[128,128]{1,0:T(8,128)S(1)}, f32[128,128]{1,0:T(8,128)S(1)}, u32[]{:S(2)}, u32[]{:S(2)}) collective-permute-start(f32[128,128]{1,0:T(8,128)S(1)} %add_add_fusion.1.a_ref), channel_id=1, source_target_pairs={{0,32},{8,40},{16,48},{24,56},{32,64},{40,72},{48,80},{56,88},{64,... | collective-permute-start | bytes 196616 | tf_op jit(solution)/shard_map/ppermute | solution.py:321
  16.3 34.7 %collective-permute-start.11 = (f32[128,128]{1,0:T(8,128)S(1)}, f32[128,128]{1,0:T(8,128)S(1)}, u32[]{:S(2)}, u32[]{:S(2)}) collective-permute-start(f32[128,128]{1,0:T(8,128)S(1)} %add_add_fusion.refs_0_), channel_id=1, source_target_pairs={{0,96},{8,104},{16,112},{24,120},{1,97},{9,105},{17,113},{25,121},... | collective-permute-start | bytes 196616 | tf_op jit(solution)/shard_map/ppermute | solution.py:350
  20.5 30.5 %collective-permute-start.10 = (f32[128,128]{1,0:T(8,128)S(1)}, f32[128,128]{1,0:T(8,128)S(1)}, u32[]{:S(2)}, u32[]{:S(2)}) collective-permute-start(f32[128,128]{1,0:T(8,128)S(1)} %add_add_fusion.refs_0_), channel_id=1, source_target_pairs={{0,64},{8,72},{16,80},{24,88},{1,65},{9,73},{17,81},{25,89},{2,66}... | collective-permute-start | bytes 196616 | tf_op jit(solution)/shard_map/ppermute | solution.py:350
  22.4 28.6 %collective-permute-start.9 = (f32[128,128]{1,0:T(8,128)S(1)}, f32[128,128]{1,0:T(8,128)S(1)}, u32[]{:S(2)}, u32[]{:S(2)}) collective-permute-start(f32[128,128]{1,0:T(8,128)S(1)} %add_add_fusion.refs_0_), channel_id=1, source_target_pairs={{0,32},{8,40},{16,48},{24,56},{1,33},{9,41},{17,49},{25,57},{2,34}... | collective-permute-start | bytes 196616 | tf_op jit(solution)/shard_map/ppermute | solution.py:350
  51.0 1.0 copy-start.2
  57.7 18.2 %all-to-all-start = ((f32[16,128,128]{2,1,0:T(8,128)}), f32[16,128,128]{2,1,0:T(8,128)S(1)}, u32[]{:S(2)}, u32[]{:S(2)}) async-start(f32[16,128,128]{2,1,0:T(8,128)} %bitcast.1), calls=%async_computation | async-start | bytes 2097152 | tf_op jit(solution)/shard_map/all_to_all | solution.py:329
  61.4 20.5 %collective-permute-start.12 = (f32[128,128]{1,0:T(8,128)S(1)}, f32[128,128]{1,0:T(8,128)S(1)}, u32[]{:S(2)}, u32[]{:S(2)}) collective-permute-start(f32[128,128]{1,0:T(8,128)S(1)} %constant_dynamic-slice_fusion), channel_id=1, source_target_pairs={{0,0},{16,1},{32,2},{48,3},{64,4},{80,5},{96,6},{112,7},{8,8},{24,... | collective-permute-start | bytes 196616 | tf_op jit(solution)/shard_map/ppermute | solution.py:355
  73.6 11.7 %copy-start.5 = (bf16[1024,128]{1,0:T(8,128)(2,1)}, bf16[1024,128]{1,0:T(8,128)(2,1)S(1)}, u32[]{:S(2)}) copy-start(bf16[1024,128]{1,0:T(8,128)(2,1)S(1)} %get-tuple-element.14.tl_ref) | copy-start | bytes 786436
  76.0 7.7 %collective-permute-start.13 = (f32[128,128]{1,0:T(8,128)S(1)}, f32[128,128]{1,0:T(8,128)S(1)}, u32[]{:S(2)}, u32[]{:S(2)}) collective-permute-start(f32[128,128]{1,0:T(8,128)S(1)} %chunk.1.w_ref), channel_id=1, source_target_pairs={{0,0},{16,1},{32,2},{48,3},{64,4},{80,5},{96,6},{112,7},{8,8},{24,... | collective-permute-start | bytes 196616 | tf_op jit(solution)/shard_map/ppermute | solution.py:361
  83.9 1.3 copy-start
  85.3 34.8 %all-to-all-start.1 = ((f32[16,128,256]{2,1,0:T(8,128)}), f32[16,128,256]{2,1,0:T(8,128)S(1)}, u32[]{:S(2)}, u32[]{:S(2)}) async-start(f32[16,128,256]{2,1,0:T(8,128)} %copy-done), calls=%async_computation.1 | async-start | bytes 4194304 | tf_op jit(solution)/shard_map/all_to_all | solution.py:329
  94.8 3.9 %collective-permute-start.14 = (f32[128,128]{1,0:T(8,128)S(1)}, f32[128,128]{1,0:T(8,128)S(1)}, u32[]{:S(2)}, u32[]{:S(2)}) collective-permute-start(f32[128,128]{1,0:T(8,128)S(1)} %collective-permute-done.13.after_ref), channel_id=1, source_target_pairs={{0,1},{1,0},{2,3},{3,2},{4,5},{5,4},{6,7},{7,6},{8,9},{9,8},{10,11... | collective-permute-start | bytes 196616 | tf_op jit(solution)/shard_map/ppermute | solution.py:364
  98.7 7.9 %collective-permute-start.17 = (f32[256,128]{1,0:T(8,128)S(1)}, f32[256,128]{1,0:T(8,128)S(1)}, u32[]{:S(2)}, u32[]{:S(2)}) collective-permute-start(f32[256,128]{1,0:T(8,128)S(1)} %pad_maximum_fusion.refs_0_), channel_id=1, source_target_pairs={{0,6},{1,7},{2,0},{3,1},{4,2},{5,3},{6,4},{7,5},{8,14},{9,15},{10,... | collective-permute-start | bytes 393224 | tf_op jit(solution)/shard_map/ppermute | solution.py:321
  101.4 5.9 %collective-permute-start.16 = (f32[256,128]{1,0:T(8,128)S(1)}, f32[256,128]{1,0:T(8,128)S(1)}, u32[]{:S(2)}, u32[]{:S(2)}) collective-permute-start(f32[256,128]{1,0:T(8,128)S(1)} %pad_maximum_fusion.refs_0_), channel_id=1, source_target_pairs={{0,4},{1,5},{2,6},{3,7},{4,0},{5,1},{6,2},{7,3},{8,12},{9,13},{10,... | collective-permute-start | bytes 393224 | tf_op jit(solution)/shard_map/ppermute | solution.py:321
  102.1 9.0 %collective-permute-start.15 = (f32[256,128]{1,0:T(8,128)S(1)}, f32[256,128]{1,0:T(8,128)S(1)}, u32[]{:S(2)}, u32[]{:S(2)}) collective-permute-start(f32[256,128]{1,0:T(8,128)S(1)} %pad_maximum_fusion.refs_0_), channel_id=1, source_target_pairs={{0,2},{1,3},{2,4},{3,5},{4,6},{5,7},{6,0},{7,1},{8,10},{9,11},{10,... | collective-permute-start | bytes 393224 | tf_op jit(solution)/shard_map/ppermute | solution.py:321
  111.8 0.9 copy-start.4
  113.6 0.9 copy-start.10
  114.5 0.9 copy-start.12
  120.7 6.7 %collective-permute-start.18 = (f32[128,128]{1,0:T(8,128)S(1)}, f32[128,128]{1,0:T(8,128)S(1)}, u32[]{:S(2)}, u32[]{:S(2)}) collective-permute-start(f32[128,128]{1,0:T(8,128)S(1)} %small.1), channel_id=1, source_target_pairs={{0,1},{1,0},{2,3},{3,2},{4,5},{5,4},{6,7},{7,6},{8,9},{9,8},{10,11... | collective-permute-start | bytes 196616 | tf_op jit(solution)/shard_map/ppermute | solution.py:369
  127.4 3.2 %collective-permute-start.21 = (f32[128,128]{1,0:T(8,128)S(1)}, f32[128,128]{1,0:T(8,128)S(1)}, u32[]{:S(2)}, u32[]{:S(2)}) collective-permute-start(f32[128,128]{1,0:T(8,128)S(1)} %add.37.refs_0_), channel_id=1, source_target_pairs={{0,6},{1,7},{2,0},{3,1},{4,2},{5,3},{6,4},{7,5},{8,14},{9,15},{10,... | collective-permute-start | bytes 196616 | tf_op jit(solution)/shard_map/ppermute | solution.py:321
  128.6 4.6 %collective-permute-start.20 = (f32[128,128]{1,0:T(8,128)S(1)}, f32[128,128]{1,0:T(8,128)S(1)}, u32[]{:S(2)}, u32[]{:S(2)}) collective-permute-start(f32[128,128]{1,0:T(8,128)S(1)} %add.37.refs_0_), channel_id=1, source_target_pairs={{0,4},{1,5},{2,6},{3,7},{4,0},{5,1},{6,2},{7,3},{8,12},{9,13},{10,... | collective-permute-start | bytes 196616 | tf_op jit(solution)/shard_map/ppermute | solution.py:321
  130.1 5.1 %collective-permute-start.19 = (f32[128,128]{1,0:T(8,128)S(1)}, f32[128,128]{1,0:T(8,128)S(1)}, u32[]{:S(2)}, u32[]{:S(2)}) collective-permute-start(f32[128,128]{1,0:T(8,128)S(1)} %add.37.refs_0_), channel_id=1, source_target_pairs={{0,2},{1,3},{2,4},{3,5},{4,6},{5,7},{6,0},{7,1},{8,10},{9,11},{10,... | collective-permute-start | bytes 196616 | tf_op jit(solution)/shard_map/ppermute | solution.py:321
  135.2 1.0 copy-start.6
  (5 other events, 3.5 us)

commit v4 on v3

--- a/solution.py
+++ b/solution.py
@@ -194,7 +194,7 @@
             copies_ref[k, :, B:] = v_ref[...]
 
     return pl.pallas_call(
-        body, out_shape=shaped(count, B, 2 * B), in_specs=[VMEM, VMEM, ANY], compiler_params=params(), name="copies"
+        body, out_shape=shaped(count, B, 2 * B), in_specs=[VMEM, VMEM, ANY], compiler_params=pltpu.CompilerParams(vmem_limit_bytes=59 * 1024 * 1024), name="copies"
     )(w, v, after)
 
 

time: 146 us -> 148 us (1.014)
  Pallas kernels: 49.5 us -> 51.7 us
    pallas_call x1, Pallas kernels: 0.18 us -> 2.37 us  [copies_kernel(): pl.pallas_call(body, out_shape=shaped(count, B, 2 * B), in_specs=[VMEM, V...]
    unnamed x26 -> x30, local copies, waits for them, and re-layouts: 10.6 us -> 9.88 us
  transfers between devices with their start and end apart: 24 -> 24, of which waited for: 11 -> 11; matrix products, arithmetic and copies ran while one was open for 1% -> 2% of each run, Pallas kernels for 23% -> 22%
where the time goes in v4:
time: 148 us; the launch traced here: 147 us
  starting transfers between devices  62 us (42%)
  Pallas kernels  51.7 us (35%)
  waiting for transfers between devices  20 us (14%)
  local copies, waits for them, and re-layouts  9.89 us (7%)
  other arithmetic  2.67 us (2%)
    pallas_call x1, Pallas kernels, factor_kernel(): pl.pallas_call(body, out_shape=(square, square), scratch_shapes=[pltpu.VM...  27.3 us
    ppermute x12, starting transfers between devices, four(): return [value] + [lax.ppermute(value, axis, along(d)) for d in (1, 2, 3)]  13.9 us
    all_to_all x2, starting transfers between devices, to_all(): return lax.all_to_all(copies, axis, split_axis=0, concat_axis=0, tiled=True)  13.2 us
    ppermute x12, waiting for transfers between devices, four(): return [value] + [lax.ppermute(value, axis, along(d)) for d in (1, 2, 3)]  11 us
    unnamed x30, local copies, waits for them, and re-layouts  9.88 us
    pallas_call x1, Pallas kernels, update_kernel(): pl.pallas_call(body, grid=(rows // tile,), out_shape=shaped(rows, cols),...  9.55 us
    ppermute x1, starting transfers between devices, shards(): lax.ppermute(lax.dynamic_slice_in_dim(v, j * B, B, 0), ('prow', 'pcol'),...  7.64 us
    ppermute x3, starting transfers between devices, shards(): lax.ppermute(top, 'prow', [(k, z * XN + k) for k in range(XN)])  7.37 us
  transfers between devices with their start and end apart: 24, of which 11 were waited for; matrix products, arithmetic and copies ran while one was open for 2% of the time, Pallas kernels for 22%

profile of v4, /device:TPU:1, one launch (start us, length us, event | category | flops | bytes accessed | tf_op | source)
XLA Modules:
  0.0 147.2 jit_solution(16257609707383807074)
XLA Ops:
  0.6 1.0 copy-done
  2.3 3.4 %collective-permute-start.2 = (f32[128,128]{1,0:T(8,128)S(1)}, f32[128,128]{1,0:T(8,128)S(1)}, u32[]{:S(2)}, u32[]{:S(2)}) collective-permute-start(f32[128,128]{1,0:T(8,128)S(1)} %gram.1), channel_id=1, source_target_pairs={{0,24},{8,0},{16,8},{24,16},{32,56},{40,32},{48,40},{56,48},{64,88... | collective-permute-start | bytes 196616 | tf_op jit(solution)/shard_map/ppermute | solution.py:321
  5.7 1.7 %collective-permute-start = (f32[128,128]{1,0:T(8,128)S(1)}, f32[128,128]{1,0:T(8,128)S(1)}, u32[]{:S(2)}, u32[]{:S(2)}) collective-permute-start(f32[128,128]{1,0:T(8,128)S(1)} %gram.1), channel_id=1, source_target_pairs={{0,16},{8,24},{16,0},{24,8},{32,48},{40,56},{48,32},{56,40},{64,80... | collective-permute-start | bytes 196616 | tf_op jit(solution)/shard_map/ppermute | solution.py:321
  8.3 2.8 %collective-permute-start.8 = (f32[128,128]{1,0:T(8,128)S(1)}, f32[128,128]{1,0:T(8,128)S(1)}, u32[]{:S(2)}, u32[]{:S(2)}) collective-permute-start(f32[128,128]{1,0:T(8,128)S(1)} %slice_select_fusion), channel_id=1, source_target_pairs={{0,24},{1,25},{2,26},{3,27},{4,28},{5,29},{6,30},{7,31}} | collective-permute-start | bytes 196616 | tf_op jit(solution)/shard_map/ppermute | solution.py:348
  11.1 1.3 collective-permute-start.7
  12.4 1.3 collective-permute-start.6
  16.3 4.2 %collective-permute-start.11 = (f32[128,128]{1,0:T(8,128)S(1)}, f32[128,128]{1,0:T(8,128)S(1)}, u32[]{:S(2)}, u32[]{:S(2)}) collective-permute-start(f32[128,128]{1,0:T(8,128)S(1)} %add_add_fusion.refs_0_), channel_id=1, source_target_pairs={{0,96},{8,104},{16,112},{24,120},{1,97},{9,105},{17,113},{25,121},... | collective-permute-start | bytes 196616 | tf_op jit(solution)/shard_map/ppermute | solution.py:350
  20.5 1.8 %collective-permute-start.10 = (f32[128,128]{1,0:T(8,128)S(1)}, f32[128,128]{1,0:T(8,128)S(1)}, u32[]{:S(2)}, u32[]{:S(2)}) collective-permute-start(f32[128,128]{1,0:T(8,128)S(1)} %add_add_fusion.refs_0_), channel_id=1, source_target_pairs={{0,64},{8,72},{16,80},{24,88},{1,65},{9,73},{17,81},{25,89},{2,66}... | collective-permute-start | bytes 196616 | tf_op jit(solution)/shard_map/ppermute | solution.py:350
  22.4 1.3 collective-permute-start.9
  23.7 27.3 %factor.1 = (f32[128,128]{1,0:T(8,128)}, f32[128,128]{1,0:T(8,128)S(1)}) custom-call(f32[128,128]{1,0:T(8,128)S(1)} %add_add_fusion.1.a_ref, f32[128,128]{1,0:T(8,128)S(1)} %collective-permute-done.3.b_ref, f32[128,128]{1,0:T(8,128)S(1)} %collective-permute-done.4.c_ref, f32[128,128]{1,0:T(8,128)S(1)} %collective-permute-done.5.d_ref), custom_call_target="tpu_custom_call" | custom-call | tf_op jit(solution)/shard_map/factor/pallas_call | solution.py:167
  51.0 1.0 copy-done.1
  52.0 5.6 %product.1 = (f32[1024,128]{1,0:T(8,128)S(1)}, f32[8,2,128,128]{3,2,1,0:T(8,128)}) custom-call(s32[1]{0:T(128)} %bitcast.first_ref, f32[1024,128]{1,0:T(8,128)S(1)} %copy-done.1, f32[128,128]{1,0:T(8,128)S(1)} %get-tuple-element.9.r_ref.refs_4_, f32[1024,2048]{1,0:T(8,128)} %a_ref.3, f32[128,128]{1,0:T(8,128)S(1)} %add_add_fusion.refs_0_, ...), custom_call_target="tpu_custom_call" | custom-call | flops 1610612736 | bytes 8388608 | tf_op jit(solution)/shard_map/product/pallas_call | solution.py:135
  57.7 3.7 %all-to-all-start = ((f32[16,128,128]{2,1,0:T(8,128)}), f32[16,128,128]{2,1,0:T(8,128)S(1)}, u32[]{:S(2)}, u32[]{:S(2)}) async-start(f32[16,128,128]{2,1,0:T(8,128)} %bitcast.1), calls=%async_computation | async-start | bytes 2097152 | tf_op jit(solution)/shard_map/all_to_all | solution.py:329
  61.4 7.6 %collective-permute-start.12 = (f32[128,128]{1,0:T(8,128)S(1)}, f32[128,128]{1,0:T(8,128)S(1)}, u32[]{:S(2)}, u32[]{:S(2)}) collective-permute-start(f32[128,128]{1,0:T(8,128)S(1)} %constant_dynamic-slice_fusion), channel_id=1, source_target_pairs={{0,0},{16,1},{32,2},{48,3},{64,4},{80,5},{96,6},{112,7},{8,8},{24,... | collective-permute-start | bytes 196616 | tf_op jit(solution)/shard_map/ppermute | solution.py:355
  69.0 4.2 %coupling.1.t_ref = f32[128,128]{1,0:T(8,128)S(1)} custom-call(f32[128,128]{1,0:T(8,128)S(1)} %add_add_fusion.refs_0_, f32[128,128]{1,0:T(8,128)S(1)} %collective-permute-done.9.refs_1_, f32[128,128]{1,0:T(8,128)S(1)} %collective-permute-done.10.refs_2_, f32[128,128]{1,0:T(8,128)S(1)} %collective-permute-done.11.refs_3_, ...), custom_call_target="tpu_custom_call" | custom-call | tf_op jit(solution)/shard_map/coupling/pallas_call | solution.py:240
  73.6 2.3 %all-to-all-done.y_ref = f32[16,128,128]{2,1,0:T(8,128)S(1)} async-done(((f32[16,128,128]{2,1,0:T(8,128)}), f32[16,128,128]{2,1,0:T(8,128)S(1)}, u32[]{:S(2)}, u32[]{:S(2)}) %all-to-all-start) | async-done | bytes 1048608 | tf_op jit(solution)/shard_map/all_to_all | solution.py:329
  76.0 5.8 %collective-permute-start.13 = (f32[128,128]{1,0:T(8,128)S(1)}, f32[128,128]{1,0:T(8,128)S(1)}, u32[]{:S(2)}, u32[]{:S(2)}) collective-permute-start(f32[128,128]{1,0:T(8,128)S(1)} %chunk.1.w_ref), channel_id=1, source_target_pairs={{0,0},{16,1},{32,2},{48,3},{64,4},{80,5},{96,6},{112,7},{8,8},{24,... | collective-permute-start | bytes 196616 | tf_op jit(solution)/shard_map/ppermute | solution.py:361
  81.8 1.9 %collective-permute-done.13.after_ref = f32[128,128]{1,0:T(8,128)S(1)} collective-permute-done((f32[128,128]{1,0:T(8,128)S(1)}, f32[128,128]{1,0:T(8,128)S(1)}, u32[]{:S(2)}, u32[]{:S(2)}) %collective-permute-start.13) | collective-permute-done | bytes 65568 | tf_op jit(solution)/shard_map/ppermute | solution.py:361
  84.4 2.4 %copies.1 = f32[16,128,256]{2,1,0:T(8,128)} custom-call(f32[128,128]{1,0:T(8,128)} %copy-done.6, f32[128,128]{1,0:T(8,128)} %copy-done.14, f32[128,128]{1,0:T(8,128)} %copy-done.13), custom_call_target="tpu_custom_call" | custom-call | tf_op jit(solution)/shard_map/copies/pallas_call | solution.py:196
  86.8 9.5 %all-to-all-start.1 = ((f32[16,128,256]{2,1,0:T(8,128)}), f32[16,128,256]{2,1,0:T(8,128)S(1)}, u32[]{:S(2)}, u32[]{:S(2)}) async-start(f32[16,128,256]{2,1,0:T(8,128)} %copies.1), calls=%async_computation.1 | async-start | bytes 4194304 | tf_op jit(solution)/shard_map/all_to_all | solution.py:329
  96.3 3.0 %collective-permute-start.14 = (f32[128,128]{1,0:T(8,128)}, f32[128,128]{1,0:T(8,128)S(1)}, u32[]{:S(2)}, u32[]{:S(2)}) collective-permute-start(f32[128,128]{1,0:T(8,128)} %copy-done.13), channel_id=1, source_target_pairs={{0,1},{1,0},{2,3},{3,2},{4,5},{5,4},{6,7},{7,6},{8,9},{9,8},{10,11... | collective-permute-start | bytes 196616 | tf_op jit(solution)/shard_map/ppermute | solution.py:364
  99.3 1.1 collective-permute-done.14
  101.2 2.7 %collective-permute-start.17 = (f32[256,128]{1,0:T(8,128)S(1)}, f32[256,128]{1,0:T(8,128)S(1)}, u32[]{:S(2)}, u32[]{:S(2)}) collective-permute-start(f32[256,128]{1,0:T(8,128)S(1)} %pad_maximum_fusion.refs_0_), channel_id=1, source_target_pairs={{0,6},{1,7},{2,0},{3,1},{4,2},{5,3},{6,4},{7,5},{8,14},{9,15},{10,... | collective-permute-start | bytes 393224 | tf_op jit(solution)/shard_map/ppermute | solution.py:321
  106.0 3.1 %collective-permute-done.17.refs_3_ = f32[256,128]{1,0:T(8,128)S(1)} collective-permute-done((f32[256,128]{1,0:T(8,128)S(1)}, f32[256,128]{1,0:T(8,128)S(1)}, u32[]{:S(2)}, u32[]{:S(2)}) %collective-permute-start.17) | collective-permute-done | bytes 131104 | tf_op jit(solution)/shard_map/ppermute | solution.py:321
  110.5 3.2 %collective-permute-done.15.refs_1_ = f32[256,128]{1,0:T(8,128)S(1)} collective-permute-done((f32[256,128]{1,0:T(8,128)S(1)}, f32[256,128]{1,0:T(8,128)S(1)}, u32[]{:S(2)}, u32[]{:S(2)}) %collective-permute-start.15) | collective-permute-done | bytes 131104 | tf_op jit(solution)/shard_map/ppermute | solution.py:321
  118.8 2.7 %all-to-all-done.1 = f32[16,128,256]{2,1,0:T(8,128)S(1)} async-done(((f32[16,128,256]{2,1,0:T(8,128)}), f32[16,128,256]{2,1,0:T(8,128)S(1)}, u32[]{:S(2)}, u32[]{:S(2)}) %all-to-all-start.1) | async-done | bytes 2097184 | tf_op jit(solution)/shard_map/all_to_all | solution.py:329
  122.2 5.8 %collective-permute-start.18 = (f32[128,128]{1,0:T(8,128)S(1)}, f32[128,128]{1,0:T(8,128)S(1)}, u32[]{:S(2)}, u32[]{:S(2)}) collective-permute-start(f32[128,128]{1,0:T(8,128)S(1)} %small.1), channel_id=1, source_target_pairs={{0,1},{1,0},{2,3},{3,2},{4,5},{5,4},{6,7},{7,6},{8,9},{9,8},{10,11... | collective-permute-start | bytes 196616 | tf_op jit(solution)/shard_map/ppermute | solution.py:369
  128.9 1.2 collective-permute-start.21
  130.1 1.5 %collective-permute-start.20 = (f32[128,128]{1,0:T(8,128)S(1)}, f32[128,128]{1,0:T(8,128)S(1)}, u32[]{:S(2)}, u32[]{:S(2)}) collective-permute-start(f32[128,128]{1,0:T(8,128)S(1)} %add.37.refs_0_), channel_id=1, source_target_pairs={{0,4},{1,5},{2,6},{3,7},{4,0},{5,1},{6,2},{7,3},{8,12},{9,13},{10,... | collective-permute-start | bytes 196616 | tf_op jit(solution)/shard_map/ppermute | solution.py:321
  132.1 2.6 %collective-permute-done.20.refs_2_ = f32[128,128]{1,0:T(8,128)S(1)} collective-permute-done((f32[128,128]{1,0:T(8,128)S(1)}, f32[128,128]{1,0:T(8,128)S(1)}, u32[]{:S(2)}, u32[]{:S(2)}) %collective-permute-start.20) | collective-permute-done | bytes 65568 | tf_op jit(solution)/shard_map/ppermute | solution.py:321
  134.7 2.0 %collective-permute-done.19.refs_1_ = f32[128,128]{1,0:T(8,128)S(1)} collective-permute-done((f32[128,128]{1,0:T(8,128)S(1)}, f32[128,128]{1,0:T(8,128)S(1)}, u32[]{:S(2)}, u32[]{:S(2)}) %collective-permute-start.19) | collective-permute-done | bytes 65568 | tf_op jit(solution)/shard_map/ppermute | solution.py:321
  137.6 9.6 %update.1 = f32[1024,2048]{1,0:T(8,128)} custom-call(f32[1024,2048]{1,0:T(8,128)} %a_ref.3, f32[8,2,128,256]{3,2,1,0:T(8,128)S(1)} %bitcast.6, f32[1024,128]{1,0:T(8,128)S(1)} %get-tuple-element.11.v_ref, bf16[1024,128]{1,0:T(8,128)(2,1)S(1)} %get-tuple-element.13.after_ref.th_ref, bf16[1024,128]{1,0:T(8,128)(2,1)S(1)} %copy-done.5, ...), custom_call_target="tpu_custom_call" | custom-call | flops 3221225472 | bytes 16777216 | tf_op jit(solution)/shard_map/update/pallas_call | solution.py:291
  (64 shorter events, 17.6 us)
Async XLA Ops:
  0.6 1.0 copy-start
  2.3 10.1 %collective-permute-start.2 = (f32[128,128]{1,0:T(8,128)S(1)}, f32[128,128]{1,0:T(8,128)S(1)}, u32[]{:S(2)}, u32[]{:S(2)}) collective-permute-start(f32[128,128]{1,0:T(8,128)S(1)} %gram.1), channel_id=1, source_target_pairs={{0,24},{8,0},{16,8},{24,16},{32,56},{40,32},{48,40},{56,48},{64,88... | collective-permute-start | bytes 196616 | tf_op jit(solution)/shard_map/ppermute | solution.py:321
  5.7 8.0 %collective-permute-start.1 = (f32[128,128]{1,0:T(8,128)S(1)}, f32[128,128]{1,0:T(8,128)S(1)}, u32[]{:S(2)}, u32[]{:S(2)}) collective-permute-start(f32[128,128]{1,0:T(8,128)S(1)} %gram.1), channel_id=1, source_target_pairs={{0,8},{8,16},{16,24},{24,0},{32,40},{40,48},{48,56},{56,32},{64,72... | collective-permute-start | bytes 196616 | tf_op jit(solution)/shard_map/ppermute | solution.py:321
  5.7 8.1 %collective-permute-start = (f32[128,128]{1,0:T(8,128)S(1)}, f32[128,128]{1,0:T(8,128)S(1)}, u32[]{:S(2)}, u32[]{:S(2)}) collective-permute-start(f32[128,128]{1,0:T(8,128)S(1)} %gram.1), channel_id=1, source_target_pairs={{0,16},{8,24},{16,0},{24,8},{32,48},{40,56},{48,32},{56,40},{64,80... | collective-permute-start | bytes 196616 | tf_op jit(solution)/shard_map/ppermute | solution.py:321
  8.3 6.4 %collective-permute-start.8 = (f32[128,128]{1,0:T(8,128)S(1)}, f32[128,128]{1,0:T(8,128)S(1)}, u32[]{:S(2)}, u32[]{:S(2)}) collective-permute-start(f32[128,128]{1,0:T(8,128)S(1)} %slice_select_fusion), channel_id=1, source_target_pairs={{0,24},{1,25},{2,26},{3,27},{4,28},{5,29},{6,30},{7,31}} | collective-permute-start | bytes 196616 | tf_op jit(solution)/shard_map/ppermute | solution.py:348
  11.1 4.3 %collective-permute-start.7 = (f32[128,128]{1,0:T(8,128)S(1)}, f32[128,128]{1,0:T(8,128)S(1)}, u32[]{:S(2)}, u32[]{:S(2)}) collective-permute-start(f32[128,128]{1,0:T(8,128)S(1)} %slice_select_fusion), channel_id=1, source_target_pairs={{0,16},{1,17},{2,18},{3,19},{4,20},{5,21},{6,22},{7,23}} | collective-permute-start | bytes 196616 | tf_op jit(solution)/shard_map/ppermute | solution.py:348
  12.4 3.0 %collective-permute-start.6 = (f32[128,128]{1,0:T(8,128)S(1)}, f32[128,128]{1,0:T(8,128)S(1)}, u32[]{:S(2)}, u32[]{:S(2)}) collective-permute-start(f32[128,128]{1,0:T(8,128)S(1)} %slice_select_fusion), channel_id=1, source_target_pairs={{0,8},{1,9},{2,10},{3,11},{4,12},{5,13},{6,14},{7,15}} | collective-permute-start | bytes 196616 | tf_op jit(solution)/shard_map/ppermute | solution.py:348
  13.8 8.6 %collective-permute-start.5 = (f32[128,128]{1,0:T(8,128)S(1)}, f32[128,128]{1,0:T(8,128)S(1)}, u32[]{:S(2)}, u32[]{:S(2)}) collective-permute-start(f32[128,128]{1,0:T(8,128)S(1)} %add_add_fusion.1.a_ref), channel_id=1, source_target_pairs={{0,96},{8,104},{16,112},{24,120},{32,0},{40,8},{48,16},{56,24},{64... | collective-permute-start | bytes 196616 | tf_op jit(solution)/shard_map/ppermute | solution.py:321
  14.7 9.0 %collective-permute-start.4 = (f32[128,128]{1,0:T(8,128)S(1)}, f32[128,128]{1,0:T(8,128)S(1)}, u32[]{:S(2)}, u32[]{:S(2)}) collective-permute-start(f32[128,128]{1,0:T(8,128)S(1)} %add_add_fusion.1.a_ref), channel_id=1, source_target_pairs={{0,64},{8,72},{16,80},{24,88},{32,96},{40,104},{48,112},{56,120},{... | collective-permute-start | bytes 196616 | tf_op jit(solution)/shard_map/ppermute | solution.py:321
  14.7 9.0 %collective-permute-start.3 = (f32[128,128]{1,0:T(8,128)S(1)}, f32[128,128]{1,0:T(8,128)S(1)}, u32[]{:S(2)}, u32[]{:S(2)}) collective-permute-start(f32[128,128]{1,0:T(8,128)S(1)} %add_add_fusion.1.a_ref), channel_id=1, source_target_pairs={{0,32},{8,40},{16,48},{24,56},{32,64},{40,72},{48,80},{56,88},{64,... | collective-permute-start | bytes 196616 | tf_op jit(solution)/shard_map/ppermute | solution.py:321
  16.3 34.7 %collective-permute-start.11 = (f32[128,128]{1,0:T(8,128)S(1)}, f32[128,128]{1,0:T(8,128)S(1)}, u32[]{:S(2)}, u32[]{:S(2)}) collective-permute-start(f32[128,128]{1,0:T(8,128)S(1)} %add_add_fusion.refs_0_), channel_id=1, source_target_pairs={{0,96},{8,104},{16,112},{24,120},{1,97},{9,105},{17,113},{25,121},... | collective-permute-start | bytes 196616 | tf_op jit(solution)/shard_map/ppermute | solution.py:350
  20.5 30.5 %collective-permute-start.10 = (f32[128,128]{1,0:T(8,128)S(1)}, f32[128,128]{1,0:T(8,128)S(1)}, u32[]{:S(2)}, u32[]{:S(2)}) collective-permute-start(f32[128,128]{1,0:T(8,128)S(1)} %add_add_fusion.refs_0_), channel_id=1, source_target_pairs={{0,64},{8,72},{16,80},{24,88},{1,65},{9,73},{17,81},{25,89},{2,66}... | collective-permute-start | bytes 196616 | tf_op jit(solution)/shard_map/ppermute | solution.py:350
  22.4 28.6 %collective-permute-start.9 = (f32[128,128]{1,0:T(8,128)S(1)}, f32[128,128]{1,0:T(8,128)S(1)}, u32[]{:S(2)}, u32[]{:S(2)}) collective-permute-start(f32[128,128]{1,0:T(8,128)S(1)} %add_add_fusion.refs_0_), channel_id=1, source_target_pairs={{0,32},{8,40},{16,48},{24,56},{1,33},{9,41},{17,49},{25,57},{2,34}... | collective-permute-start | bytes 196616 | tf_op jit(solution)/shard_map/ppermute | solution.py:350
  51.0 1.0 copy-start.1
  57.7 18.2 %all-to-all-start = ((f32[16,128,128]{2,1,0:T(8,128)}), f32[16,128,128]{2,1,0:T(8,128)S(1)}, u32[]{:S(2)}, u32[]{:S(2)}) async-start(f32[16,128,128]{2,1,0:T(8,128)} %bitcast.1), calls=%async_computation | async-start | bytes 2097152 | tf_op jit(solution)/shard_map/all_to_all | solution.py:329
  61.4 20.5 %collective-permute-start.12 = (f32[128,128]{1,0:T(8,128)S(1)}, f32[128,128]{1,0:T(8,128)S(1)}, u32[]{:S(2)}, u32[]{:S(2)}) collective-permute-start(f32[128,128]{1,0:T(8,128)S(1)} %constant_dynamic-slice_fusion), channel_id=1, source_target_pairs={{0,0},{16,1},{32,2},{48,3},{64,4},{80,5},{96,6},{112,7},{8,8},{24,... | collective-permute-start | bytes 196616 | tf_op jit(solution)/shard_map/ppermute | solution.py:355
  73.6 13.2 %copy-start.4 = (bf16[1024,128]{1,0:T(8,128)(2,1)}, bf16[1024,128]{1,0:T(8,128)(2,1)S(1)}, u32[]{:S(2)}) copy-start(bf16[1024,128]{1,0:T(8,128)(2,1)S(1)} %get-tuple-element.14.tl_ref) | copy-start | bytes 786436
  76.0 7.8 %copy-start.6 = (f32[128,128]{1,0:T(8,128)}, f32[128,128]{1,0:T(8,128)S(1)}, u32[]{:S(2)}) copy-start(f32[128,128]{1,0:T(8,128)S(1)} %chunk.1.w_ref) | copy-start | bytes 196612
  76.0 7.7 %collective-permute-start.13 = (f32[128,128]{1,0:T(8,128)S(1)}, f32[128,128]{1,0:T(8,128)S(1)}, u32[]{:S(2)}, u32[]{:S(2)}) collective-permute-start(f32[128,128]{1,0:T(8,128)S(1)} %chunk.1.w_ref), channel_id=1, source_target_pairs={{0,0},{16,1},{32,2},{48,3},{64,4},{80,5},{96,6},{112,7},{8,8},{24,... | collective-permute-start | bytes 196616 | tf_op jit(solution)/shard_map/ppermute | solution.py:361
  81.8 1.9 %copy-start.14 = (f32[128,128]{1,0:T(8,128)}, f32[128,128]{1,0:T(8,128)S(1)}, u32[]{:S(2)}) copy-start(f32[128,128]{1,0:T(8,128)S(1)} %collective-permute-done.12.v_ref) | copy-start | bytes 196612
  86.8 34.8 %all-to-all-start.1 = ((f32[16,128,256]{2,1,0:T(8,128)}), f32[16,128,256]{2,1,0:T(8,128)S(1)}, u32[]{:S(2)}, u32[]{:S(2)}) async-start(f32[16,128,256]{2,1,0:T(8,128)} %copies.1), calls=%async_computation.1 | async-start | bytes 4194304 | tf_op jit(solution)/shard_map/all_to_all | solution.py:329
  96.3 4.1 %collective-permute-start.14 = (f32[128,128]{1,0:T(8,128)}, f32[128,128]{1,0:T(8,128)S(1)}, u32[]{:S(2)}, u32[]{:S(2)}) collective-permute-start(f32[128,128]{1,0:T(8,128)} %copy-done.13), channel_id=1, source_target_pairs={{0,1},{1,0},{2,3},{3,2},{4,5},{5,4},{6,7},{7,6},{8,9},{9,8},{10,11... | collective-permute-start | bytes 196616 | tf_op jit(solution)/shard_map/ppermute | solution.py:364
  101.2 7.9 %collective-permute-start.17 = (f32[256,128]{1,0:T(8,128)S(1)}, f32[256,128]{1,0:T(8,128)S(1)}, u32[]{:S(2)}, u32[]{:S(2)}) collective-permute-start(f32[256,128]{1,0:T(8,128)S(1)} %pad_maximum_fusion.refs_0_), channel_id=1, source_target_pairs={{0,6},{1,7},{2,0},{3,1},{4,2},{5,3},{6,4},{7,5},{8,14},{9,15},{10,... | collective-permute-start | bytes 393224 | tf_op jit(solution)/shard_map/ppermute | solution.py:321
  103.9 5.9 %collective-permute-start.16 = (f32[256,128]{1,0:T(8,128)S(1)}, f32[256,128]{1,0:T(8,128)S(1)}, u32[]{:S(2)}, u32[]{:S(2)}) collective-permute-start(f32[256,128]{1,0:T(8,128)S(1)} %pad_maximum_fusion.refs_0_), channel_id=1, source_target_pairs={{0,4},{1,5},{2,6},{3,7},{4,0},{5,1},{6,2},{7,3},{8,12},{9,13},{10,... | collective-permute-start | bytes 393224 | tf_op jit(solution)/shard_map/ppermute | solution.py:321
  104.7 9.0 %collective-permute-start.15 = (f32[256,128]{1,0:T(8,128)S(1)}, f32[256,128]{1,0:T(8,128)S(1)}, u32[]{:S(2)}, u32[]{:S(2)}) collective-permute-start(f32[256,128]{1,0:T(8,128)S(1)} %pad_maximum_fusion.refs_0_), channel_id=1, source_target_pairs={{0,2},{1,3},{2,4},{3,5},{4,6},{5,7},{6,0},{7,1},{8,10},{9,11},{10,... | collective-permute-start | bytes 393224 | tf_op jit(solution)/shard_map/ppermute | solution.py:321
  114.3 0.9 copy-start.3
  115.2 0.9 copy-start.8
  122.2 6.7 %collective-permute-start.18 = (f32[128,128]{1,0:T(8,128)S(1)}, f32[128,128]{1,0:T(8,128)S(1)}, u32[]{:S(2)}, u32[]{:S(2)}) collective-permute-start(f32[128,128]{1,0:T(8,128)S(1)} %small.1), channel_id=1, source_target_pairs={{0,1},{1,0},{2,3},{3,2},{4,5},{5,4},{6,7},{7,6},{8,9},{9,8},{10,11... | collective-permute-start | bytes 196616 | tf_op jit(solution)/shard_map/ppermute | solution.py:369
  128.9 3.2 %collective-permute-start.21 = (f32[128,128]{1,0:T(8,128)S(1)}, f32[128,128]{1,0:T(8,128)S(1)}, u32[]{:S(2)}, u32[]{:S(2)}) collective-permute-start(f32[128,128]{1,0:T(8,128)S(1)} %add.37.refs_0_), channel_id=1, source_target_pairs={{0,6},{1,7},{2,0},{3,1},{4,2},{5,3},{6,4},{7,5},{8,14},{9,15},{10,... | collective-permute-start | bytes 196616 | tf_op jit(solution)/shard_map/ppermute | solution.py:321
  130.1 4.6 %collective-permute-start.20 = (f32[128,128]{1,0:T(8,128)S(1)}, f32[128,128]{1,0:T(8,128)S(1)}, u32[]{:S(2)}, u32[]{:S(2)}) collective-permute-start(f32[128,128]{1,0:T(8,128)S(1)} %add.37.refs_0_), channel_id=1, source_target_pairs={{0,4},{1,5},{2,6},{3,7},{4,0},{5,1},{6,2},{7,3},{8,12},{9,13},{10,... | collective-permute-start | bytes 196616 | tf_op jit(solution)/shard_map/ppermute | solution.py:321
  131.6 5.1 %collective-permute-start.19 = (f32[128,128]{1,0:T(8,128)S(1)}, f32[128,128]{1,0:T(8,128)S(1)}, u32[]{:S(2)}, u32[]{:S(2)}) collective-permute-start(f32[128,128]{1,0:T(8,128)S(1)} %add.37.refs_0_), channel_id=1, source_target_pairs={{0,2},{1,3},{2,4},{3,5},{4,6},{5,7},{6,0},{7,1},{8,10},{9,11},{10,... | collective-permute-start | bytes 196616 | tf_op jit(solution)/shard_map/ppermute | solution.py:321
  136.7 1.0 copy-start.5
  (7 other events, 5.0 us)
